TPU v7x, 32 devices: a whole 2x2x4 slice. The times are simulated.
32 devices in a mesh: section: 2 (over core), batch: 4 (over z), mp: 4 (over y, x).
Axes of the slice: x: 2, y: 2, z: 4, core: 2. Of those that a mesh axis runs over, the one named last changes fastest.
Arguments:
- encoder_in: bfloat16 [4, 6, 256, 768], P('batch', None, 'mp'), may hold values from -6 to 6
- context_lengths: int32 [4, 6, 4], P('batch'), may hold values from 1 to 128, 256 in all within a row
- target_lengths: int32 [4, 6, 4], P('batch'), may hold values from 1 to 64, 128 in all within a row
- target_places: int32 [4, 6, 128], P('batch', None, 'mp'), may hold values from 0 to 783
- encoder_norm1: float32 [768], replicated, may hold values from 0.25 to 1.75
- encoder_qkv: bfloat16 [3, 768, 768], P(None, None, 'mp'), may hold values from -0.21875 to 0.21875
- encoder_proj: bfloat16 [768, 768], P('mp'), may hold values from -1.25 to 1.25
- encoder_norm2: float32 [768], replicated, may hold values from 0.25 to 1.75
- encoder_up: bfloat16 [768, 3072], P(None, 'mp'), may hold values from -0.21875 to 0.21875
- encoder_down: bfloat16 [3072, 768], P('mp'), may hold values from -0.109375 to 0.109375
- link_weight: bfloat16 [768, 384], replicated, may hold values from -0.21875 to 0.21875
- mask_token: float32 [384], replicated, may hold values from -4 to 4
- predictor_norm1: float32 [384], replicated, may hold values from 0.25 to 1.75
- predictor_qkv: bfloat16 [3, 384, 384], P(None, None, 'mp'), may hold values from -0.3125 to 0.3125
- predictor_proj: bfloat16 [384, 384], P('mp'), may hold values from -1.75 to 1.75
- predictor_norm2: float32 [384], replicated, may hold values from 0.25 to 1.75
- predictor_up: bfloat16 [384, 1536], P(None, 'mp'), may hold values from -0.3125 to 0.3125
- predictor_down: bfloat16 [1536, 384], P('mp'), may hold values from -0.15625 to 0.15625
- cotangent: bfloat16 [4, 6, 128, 384], P('batch', None, 'mp'), may hold values from -6 to 6
Outputs:
- encoder_in_grad: float32 [4, 6, 256, 768], P('batch', 'section', 'mp')
- encoder_norm1_grad: float32 [768], replicated
- encoder_qkv_grad: float32 [3, 768, 768], P(None, ('section', 'batch'), 'mp')
- encoder_proj_grad: float32 [768, 768], P('mp', ('section', 'batch'))
- encoder_norm2_grad: float32 [768], replicated
- encoder_up_grad: float32 [768, 3072], P(('section', 'batch'), 'mp')
- encoder_down_grad: float32 [3072, 768], P('mp', ('section', 'batch'))
- link_grad: float32 [768, 384], replicated
- mask_grad: float32 [384], replicated
- predictor_norm1_grad: float32 [384], replicated
- predictor_qkv_grad: float32 [3, 384, 384], P(None, ('section', 'batch'), 'mp')
- predictor_proj_grad: float32 [384, 384], P('mp', ('section', 'batch'))
- predictor_norm2_grad: float32 [384], replicated
- predictor_up_grad: float32 [384, 1536], P(('section', 'batch'), 'mp')
- predictor_down_grad: float32 [1536, 384], P('mp', ('section', 'batch'))
Inputs may be any that keep to these rules, and one draw needn't show every extreme that they name: `context_lengths`: in every micro-batch the 4 lengths sum to 256 and the longest is exactly 128. `target_lengths`: in every micro-batch the 4 lengths sum to 128 and the longest is exactly 64.
All inputs are finite; a program needn't handle non-finite values.
Results may differ from a plain program's by a relative error of at most 0.04.
Values may be sent and summed in bfloat16 or wider, within the bound.
A program may use at most 256 MiB of HBM per device.

v0:
```python
import math

import jax
import jax.numpy as jnp
from jax import lax
from jax.sharding import PartitionSpec as P

D = 768
HEADS = 12
PD = 384
PHEADS = 12
MB = 6
CAP_C = 256
CAP_T = 128


NORM_EPSILON = 1e-06


def from_behind(array, axis, by):
    length = lax.axis_size(axis)
    pairs = [(i, i + by) for i in range(length) if 0 <= i + by < length]
    return lax.ppermute(array, axis, pairs)


def layer_norm(values, gain_vec):
    average = jnp.mean(values, axis=-1, keepdims=True)
    centred = values - average
    variance = jnp.mean(centred * centred, axis=-1, keepdims=True)
    return centred * lax.rsqrt(variance + NORM_EPSILON) * gain_vec


def segment_of(lengths, length_all):
    boundary = jnp.cumsum(lengths)
    places = jnp.arange(length_all, dtype=jnp.int32)
    return jnp.sum((places[:, None] >= boundary[None, :]).astype(jnp.int32), axis=1)


def position_code(places, features):
    half_width = features // 2
    frequency = jnp.exp(
        jnp.arange(half_width, dtype=jnp.float32) * (-2.0 * math.log(10000.0) / features)
    )
    angles = places.astype(jnp.float32)[:, None] * frequency[None, :]
    return jnp.concatenate([jnp.sin(angles), jnp.cos(angles)], axis=1)


def spread_rows(values):
    return lax.all_gather(values, "mp", axis=0, tiled=True)


def collect_rows(values):
    return lax.psum_scatter(
        values.astype(jnp.bfloat16), "mp", scatter_dimension=0, tiled=True
    ).astype(jnp.float32)


def spread_grads(values):
    return lax.all_gather(values, "mp", axis=0, tiled=True)


def collect_grads(values):
    return lax.psum_scatter(
        values.astype(jnp.bfloat16), "mp", scatter_dimension=0, tiled=True
    ).astype(jnp.float32)


def pick_side(flag, first_side, second_side):
    return jax.tree.map(
        lambda left_arr, right_arr: jnp.where(flag, left_arr, right_arr), first_side, second_side
    )


def split_heads(triple, head_count):
    length_all = triple.shape[1]
    local_heads = head_count // lax.axis_size("mp")
    head_size = triple.shape[2] // local_heads
    shaped = triple.reshape(3, length_all, local_heads, head_size)
    return (shaped[0], shaped[1], shaped[2], head_size ** (-0.5))


def scores_of(queries, key_rows, allowed, scaling):
    raw_scores = (
        jnp.einsum("qhd,khd->hqk", queries, key_rows, preferred_element_type=jnp.float32) * scaling
    )
    return jnp.where(allowed[None], raw_scores, -1e30)


def gelu_exact(values):
    return jax.nn.gelu(values, approximate=False)


def block_forward(token_rows, weights, allowed, head_count, finish):
    norm_one, qkv_weight, proj_weight, norm_two, up_weight, down_weight = weights
    normed = layer_norm(token_rows, norm_one).astype(jnp.bfloat16)
    gathered = spread_rows(normed)
    triple = jnp.einsum(
        "sw,twc->tsc", gathered, qkv_weight, preferred_element_type=jnp.float32
    ).astype(jnp.bfloat16)
    queries, key_rows, value_rows, scaling = split_heads(triple, head_count)
    scores = scores_of(queries, key_rows, allowed, scaling)
    row_peak = jnp.max(scores, axis=-1, keepdims=True)
    raised = jnp.exp(scores - row_peak)
    row_mass = jnp.sum(raised, axis=-1, keepdims=True)
    log_mass = row_peak + jnp.log(row_mass)
    attn_weights = (raised / row_mass).astype(jnp.bfloat16)
    mixture = jnp.einsum(
        "hqk,khd->qhd", attn_weights, value_rows, preferred_element_type=jnp.float32
    )
    mixture = mixture.reshape(gathered.shape[0], -1).astype(jnp.bfloat16)
    midway = token_rows + collect_rows(
        jnp.dot(mixture, proj_weight, preferred_element_type=jnp.float32)
    )
    normed_two = layer_norm(midway, norm_two).astype(jnp.bfloat16)
    gathered_two = spread_rows(normed_two)
    lifted = jnp.dot(gathered_two, up_weight, preferred_element_type=jnp.float32)
    hidden = gelu_exact(lifted).astype(jnp.bfloat16)
    stored = (gathered, triple, log_mass, mixture, midway, gathered_two, lifted, hidden)
    if finish:
        return (
            midway + collect_rows(jnp.dot(hidden, down_weight, preferred_element_type=jnp.float32)),
            stored,
        )
    return (midway, stored)


def block_backward(token_rows, weights, allowed, head_count, stored, grad_out):
    norm_one, qkv_weight, proj_weight, norm_two, up_weight, down_weight = weights
    gathered, triple, log_mass, mixture, midway, gathered_two, lifted, hidden = stored
    length_all = gathered.shape[0]
    grad_branch = spread_grads(grad_out.astype(jnp.bfloat16))
    down_grad = jnp.dot(hidden.T, grad_branch, preferred_element_type=jnp.float32)
    grad_hidden = jnp.dot(grad_branch, down_weight.T, preferred_element_type=jnp.float32)
    gelu_value, gelu_pull = jax.vjp(gelu_exact, lifted)
    grad_lifted = gelu_pull(grad_hidden)[0].astype(jnp.bfloat16)
    up_grad = jnp.dot(gathered_two.T, grad_lifted, preferred_element_type=jnp.float32)
    grad_normed_two = collect_grads(
        jnp.dot(grad_lifted, up_weight.T, preferred_element_type=jnp.float32)
    )
    norm_value, norm_pull = jax.vjp(layer_norm, midway, norm_two)
    grad_midway_norm, norm_two_grad = norm_pull(grad_normed_two)
    grad_midway = grad_out + grad_midway_norm
    grad_attn = spread_grads(grad_midway.astype(jnp.bfloat16))
    proj_grad = jnp.dot(mixture.T, grad_attn, preferred_element_type=jnp.float32)
    queries, key_rows, value_rows, scaling = split_heads(triple, head_count)
    grad_mixture = jnp.dot(grad_attn, proj_weight.T, preferred_element_type=jnp.float32).astype(
        jnp.bfloat16
    )
    grad_mixture = grad_mixture.reshape(queries.shape)
    scores = scores_of(queries, key_rows, allowed, scaling)
    attn_probs = jnp.exp(scores - log_mass)
    value_grad = jnp.einsum(
        "hqk,qhd->khd",
        attn_probs.astype(jnp.bfloat16),
        grad_mixture,
        preferred_element_type=jnp.float32,
    )
    grad_probs = jnp.einsum(
        "qhd,khd->hqk", grad_mixture, value_rows, preferred_element_type=jnp.float32
    )
    grad_scores = attn_probs * (
        grad_probs - jnp.sum(attn_probs * grad_probs, axis=-1, keepdims=True)
    )
    grad_scores = grad_scores.astype(jnp.bfloat16)
    query_grad = (
        jnp.einsum("hqk,khd->qhd", grad_scores, key_rows, preferred_element_type=jnp.float32)
        * scaling
    )
    key_grad = (
        jnp.einsum("hqk,qhd->khd", grad_scores, queries, preferred_element_type=jnp.float32)
        * scaling
    )
    grad_triple = jnp.stack(
        [
            query_grad.reshape(length_all, -1),
            key_grad.reshape(length_all, -1),
            value_grad.reshape(length_all, -1),
        ]
    ).astype(jnp.bfloat16)
    qkv_grad = jnp.einsum("sw,tsc->twc", gathered, grad_triple, preferred_element_type=jnp.float32)
    grad_normed = collect_grads(
        jnp.einsum("tsc,twc->sw", grad_triple, qkv_weight, preferred_element_type=jnp.float32)
    )
    first_value, first_pull = jax.vjp(layer_norm, token_rows, norm_one)
    grad_rows_norm, norm_one_grad = first_pull(grad_normed)
    grad_rows = grad_midway + grad_rows_norm
    return (grad_rows, (norm_one_grad, qkv_grad, proj_grad, norm_two_grad, up_grad, down_grad))


def body(
    encoder_in,
    context_lengths,
    target_lengths,
    target_places,
    encoder_norm1,
    encoder_qkv,
    encoder_proj,
    encoder_norm2,
    encoder_up,
    encoder_down,
    link_weight,
    mask_token,
    predictor_norm1,
    predictor_qkv,
    predictor_proj,
    predictor_norm2,
    predictor_up,
    predictor_down,
    cotangent,
):
    encoder_weights = (
        encoder_norm1,
        encoder_qkv,
        encoder_proj,
        encoder_norm2,
        encoder_up,
        encoder_down,
    )
    predictor_weights = (
        predictor_norm1,
        predictor_qkv,
        predictor_proj,
        predictor_norm2,
        predictor_up,
        predictor_down,
    )
    mp_count = lax.axis_size("mp")
    context_rows = CAP_C // mp_count
    target_rows = CAP_T // mp_count
    on_first = lax.axis_index("section") == 0
    inputs = encoder_in[0]
    context_all = context_lengths[0]
    target_all = target_lengths[0]
    places_all = target_places[0]
    cotangent_all = cotangent[0]

    def single_zeros(arrays):
        return tuple((jnp.zeros(weight_arr.shape, jnp.float32) for weight_arr in arrays))

    def context_mask(lengths):
        segments = segment_of(lengths, CAP_C)
        return segments[:, None] == segments[None, :]

    def encode_one(token_rows, lengths):
        encoded = block_forward(
            token_rows.astype(jnp.float32), encoder_weights, context_mask(lengths), HEADS, True
        )[0]
        return encoded.astype(jnp.bfloat16)

    def predict_one(encoded, context_one, target_one, places_one, cotangent_rows):
        context = jnp.dot(encoded, link_weight, preferred_element_type=jnp.float32)
        masked = mask_token[None, :] + position_code(places_one, PD)
        token_rows = jnp.concatenate([context, masked], axis=0)
        context_segments = segment_of(context_one, CAP_C).reshape(mp_count, context_rows)
        target_segments = segment_of(target_one, CAP_T).reshape(mp_count, target_rows)
        segments = jnp.concatenate([context_segments, target_segments], axis=1).reshape(-1)
        allowed = segments[:, None] == segments[None, :]
        midway, stored = block_forward(token_rows, predictor_weights, allowed, PHEADS, False)
        grad_out = jnp.concatenate(
            [jnp.zeros((context_rows, PD), jnp.float32), cotangent_rows.astype(jnp.float32)], axis=0
        )
        grad_rows, grads = block_backward(
            token_rows, predictor_weights, allowed, PHEADS, stored, grad_out
        )
        grad_context = grad_rows[:context_rows].astype(jnp.bfloat16)
        link_part = jnp.dot(encoded.T, grad_context, preferred_element_type=jnp.float32)
        mask_part = jnp.sum(grad_rows[context_rows:], axis=0)
        grad_encoded = jnp.dot(
            grad_context, link_weight.T, preferred_element_type=jnp.float32
        ).astype(jnp.bfloat16)
        return (grad_encoded, grads, link_part, mask_part)

    def learn_one(token_rows, lengths, grad_out):
        token_rows = token_rows.astype(jnp.float32)
        allowed = context_mask(lengths)
        midway, stored = block_forward(token_rows, encoder_weights, allowed, HEADS, False)
        return block_backward(
            token_rows, encoder_weights, allowed, HEADS, stored, grad_out.astype(jnp.float32)
        )

    def tick_step(carried, tick):
        held_encoded, held_grad = carried
        ahead = jnp.minimum(tick, MB - 1)
        middle = jnp.clip(tick - 1, 0, MB - 1)
        behind = jnp.clip(tick - 2, 0, MB - 1)
        encoded = encode_one(inputs[ahead], context_all[ahead])
        grad_rows, enc_grads = learn_one(inputs[behind], context_all[behind], held_grad)
        encoder_side = (
            encoded,
            jnp.zeros((context_rows, D), jnp.bfloat16),
            grad_rows,
            enc_grads,
            single_zeros(predictor_weights),
            jnp.zeros(link_weight.shape, jnp.float32),
            jnp.zeros((PD,), jnp.float32),
        )
        grad_encoded, pred_grads, link_part, mask_part = predict_one(
            held_encoded,
            context_all[middle],
            target_all[middle],
            places_all[middle],
            cotangent_all[middle],
        )
        predictor_side = (
            jnp.zeros((context_rows, D), jnp.bfloat16),
            grad_encoded,
            jnp.zeros((context_rows, D), jnp.float32),
            single_zeros(encoder_weights),
            pred_grads,
            link_part,
            mask_part,
        )
        results = pick_side(on_first, encoder_side, predictor_side)
        sent_up = from_behind(results[0], "section", 1)
        sent_down = from_behind(results[1], "section", -1)
        return ((sent_up, sent_down), results[2:])

    start = (jnp.zeros((context_rows, D), jnp.bfloat16), jnp.zeros((context_rows, D), jnp.bfloat16))
    tick_list = jnp.arange(MB + 2, dtype=jnp.int32)
    collected = lax.scan(tick_step, start, tick_list)[1]
    grad_inputs = collected[0][2:]
    encoder_grads = tuple((part_arr[2:] for part_arr in collected[1]))
    predictor_grads = tuple((part_arr[1 : MB + 1] for part_arr in collected[2]))
    link_grads = collected[3][1 : MB + 1]
    mask_grads = collected[4][1 : MB + 1]
    half_count = MB // 2
    shipped = from_behind(grad_inputs[half_count:].astype(jnp.bfloat16), "section", 1).astype(
        jnp.float32
    )
    encoder_in_grad = jnp.where(on_first, grad_inputs[:half_count], shipped)[None]
    large_grads = (
        encoder_grads[1],
        encoder_grads[2],
        encoder_grads[4],
        encoder_grads[5],
        predictor_grads[1],
        predictor_grads[2],
        predictor_grads[4],
        predictor_grads[5],
    )
    minor_grads = (
        encoder_grads[0],
        encoder_grads[3],
        link_grads,
        mask_grads,
        predictor_grads[0],
        predictor_grads[3],
    )

    def pair_up(part_arr):
        return jnp.sum(part_arr.reshape((half_count, 2) + part_arr.shape[1:]), axis=1)

    large_pairs = tuple((pair_up(part_arr) for part_arr in large_grads))
    minor_pairs = tuple((pair_up(part_arr) for part_arr in minor_grads))

    def reduce_step(carried, element):
        large_item, minor_item = element
        large_part = (
            lax.psum_scatter(large_item[0], ("section", "batch"), scatter_dimension=1, tiled=True),
            lax.psum_scatter(large_item[1], ("section", "batch"), scatter_dimension=1, tiled=True),
            lax.psum_scatter(large_item[2], ("section", "batch"), scatter_dimension=0, tiled=True),
            lax.psum_scatter(large_item[3], ("section", "batch"), scatter_dimension=1, tiled=True),
            lax.psum_scatter(large_item[4], ("section", "batch"), scatter_dimension=1, tiled=True),
            lax.psum_scatter(large_item[5], ("section", "batch"), scatter_dimension=1, tiled=True),
            lax.psum_scatter(large_item[6], ("section", "batch"), scatter_dimension=0, tiled=True),
            lax.psum_scatter(large_item[7], ("section", "batch"), scatter_dimension=1, tiled=True),
        )
        minor_part = lax.psum(minor_item, ("section", "batch", "mp"))
        return (carried, (large_part, minor_part))

    large_parts, minor_parts = lax.scan(reduce_step, 0, (large_pairs, minor_pairs))[1]
    large_total = tuple((jnp.sum(part_arr, axis=0) for part_arr in large_parts))
    minor_total = tuple((jnp.sum(part_arr, axis=0) for part_arr in minor_parts))
    return (
        encoder_in_grad,
        minor_total[0],
        large_total[0],
        large_total[1],
        minor_total[1],
        large_total[2],
        large_total[3],
        minor_total[2],
        minor_total[3],
        minor_total[4],
        large_total[4],
        large_total[5],
        minor_total[5],
        large_total[6],
        large_total[7],
    )


def solution(mesh):
    return jax.shard_map(
        body,
        mesh=mesh,
        in_specs=(
            P("batch", None, "mp", None),
            P("batch", None, None),
            P("batch", None, None),
            P("batch", None, "mp"),
            P(),
            P(None, None, "mp"),
            P("mp", None),
            P(),
            P(None, "mp"),
            P("mp", None),
            P(),
            P(),
            P(),
            P(None, None, "mp"),
            P("mp", None),
            P(),
            P(None, "mp"),
            P("mp", None),
            P("batch", None, "mp", None),
        ),
        out_specs=(
            P("batch", "section", "mp", None),
            P(),
            P(None, ("section", "batch"), "mp"),
            P("mp", ("section", "batch")),
            P(),
            P(("section", "batch"), "mp"),
            P("mp", ("section", "batch")),
            P(),
            P(),
            P(),
            P(None, ("section", "batch"), "mp"),
            P("mp", ("section", "batch")),
            P(),
            P(("section", "batch"), "mp"),
            P("mp", ("section", "batch")),
        ),
        check_vma=False,
    )
```

profile of v0, /device:TPU:0, one launch (start us, length us, event | category | flops | bytes accessed | tf_op | source)
XLA Modules:
  0.0 3788.8 jit_solution(4045125655604860957)
XLA Ops:
  11.8 2226.6 %while.80 = (s32[]{:T(128)}, bf16[64,768]{1,0:T(8,128)(2,1)S(1)}, bf16[64,768]{1,0:T(8,128)(2,1)S(1)}, f32[8,64,768]{2,1,0:T(8,128)}, f32[8,768]{1,0:T(8,128)}, ...) while((s32[]{:T(128)}, bf16[64,768]{1,0:T(8,128)(2,1)S(1)}, ...), condition=%wide.region_50.51_spmd, body=%wide.region_0.50_spmd.sunk | while | flops 4824809984 | bytes 157825872 | solution.py:320
  19.8 10.6 all_gather.76
  77.3 10.5 all_gather.77
  170.1 20.4 reduce-scatter.37.cloned.1.call-done
  220.7 25.1 reduce-scatter.39.cloned.1.call-done
  269.7 17.3 reduce-scatter.41.cloned.1.call-done
  445.7 21.7 reduce-scatter.37.cloned.1.call-done
  497.6 24.9 reduce-scatter.39.cloned.1.call-done
  546.4 17.4 reduce-scatter.41.cloned.1.call-done
  608.2 10.4 all_gather.73
  722.5 21.5 reduce-scatter.37.cloned.1.call-done
  747.4 10.4 all_gather.74
  774.4 25.1 reduce-scatter.39.cloned.1.call-done
  823.4 17.3 reduce-scatter.41.cloned.1.call-done
  946.1 10.6 all_gather.72
  1000.4 21.8 reduce-scatter.37.cloned.1.call-done
  1052.4 25.1 reduce-scatter.39.cloned.1.call-done
  1101.4 17.3 reduce-scatter.41.cloned.1.call-done
  1277.6 21.5 reduce-scatter.37.cloned.1.call-done
  1302.4 10.4 all_gather.74
  1329.5 24.9 reduce-scatter.39.cloned.1.call-done
  1378.3 17.3 reduce-scatter.41.cloned.1.call-done
  1554.5 21.4 reduce-scatter.37.cloned.1.call-done
  1606.0 25.0 reduce-scatter.39.cloned.1.call-done
  1654.9 17.2 reduce-scatter.41.cloned.1.call-done
  1830.8 21.3 reduce-scatter.37.cloned.1.call-done
  1855.5 10.4 all_gather.74
  1882.5 25.1 reduce-scatter.39.cloned.1.call-done
  1931.5 17.3 reduce-scatter.41.cloned.1.call-done
  2054.2 10.4 all_gather.72
  2108.2 21.1 reduce-scatter.37.cloned.1.call-done
  2132.6 10.4 all_gather.74
  2159.6 24.9 reduce-scatter.39.cloned.1.call-done
  2208.5 17.3 reduce-scatter.41.cloned.1.call-done
  2242.6 11.8 slice.138
  2254.4 11.8 slice.139
  2342.9 1423.1 %while.81 = (s32[]{:T(128)}, f32[3,3,96,192]{3,2,1,0:T(8,128)}, f32[3,192,96]{2,1,0:T(8,128)}, f32[3,96,768]{2,1,0:T(8,128)}, f32[3,768,96]{2,1,0:T(8,128)}, /*i...) while((s32[]{:T(128)}, f32[3,3,96,192]{3,2,1,0:T(8,128)}, ...), condition=%wide.region_80.81_spmd, body=%wide.region_65.80_spmd.sunk | while | flops 297602 | bytes 78272224 | solution.py:371
  2366.4 39.8 %all-reduce.3 = (f32[1,768]{1,0:T(1,128)S(1)}, f32[1,768]{1,0:T(1,128)S(1)}, f32[1,384]{1,0:T(1,128)S(1)}, f32[1,384]{1,0:T(1,128)S(1)}, f32[1,384]{1,0:T(1,128)S(1)}) all-reduce(f32[1,768]{1,0:T(1,128)S(1)} %get-tuple-element.1611, ...), channel_id=1, replica_groups=mesh['section'=2,'batch'=4,'mp'=4] {'section','batch','mp'}, use_global_device_ids=true, to_apply=%region_74.74 | all-reduce | flops 2688 | bytes 21504 | tf_op jit(solution)/shard_map/while/body/eval_jaxpr/psum | solution.py:368
  2407.9 105.8 %all-reduce.6.cloned.1.call-done = f32[1,768,384]{2,1,0:T(8,128)} async-done(((f32[1,768,384]{2,1,0:T(8,128)}), f32[1,768,384]{2,1,0:T(8,128)}) %all-reduce.6.cloned.1.call-update) | async-done | bytes 1179664 | tf_op jit(solution)/shard_map/while/body/eval_jaxpr/psum | solution.py:368
  2516.0 31.5 reduce-scatter.57.cloned.1.call-done
  2549.0 32.1 reduce-scatter.63.cloned.1.call-done
  2582.1 34.2 reduce-scatter.51.cloned.1.call-done
  2617.3 32.6 reduce-scatter.61.cloned.1.call-done
  2652.8 52.3 %reduce-scatter.49.cloned.1.call-done = f32[3,96,192]{2,1,0:T(8,128)} async-done(((f32[3,768,192]{2,1,0:T(8,128)}), f32[3,96,192]{2,1,0:T(8,128)}) %reduce-scatter.49.cloned.1.call-update) | async-done | bytes 221200 | tf_op jit(solution)/shard_map/while/body/eval_jaxpr/reduce_scatter | solution.py:359
  2706.8 53.8 %reduce-scatter.55.cloned.1.call-done = f32[96,768]{1,0:T(8,128)} async-done(((f32[768,768]{1,0:T(8,128)}), f32[96,768]{1,0:T(8,128)}) %reduce-scatter.55.cloned.1.call-update) | async-done | bytes 294928 | tf_op jit(solution)/shard_map/while
  2762.5 53.6 %reduce-scatter.53.cloned.1.call-done = f32[96,768]{1,0:T(8,128)} async-done(((f32[768,768]{1,0:T(8,128)}), f32[96,768]{1,0:T(8,128)}) %reduce-scatter.53.cloned.1.call-update) | async-done | bytes 294928 | tf_op jit(solution)/shard_map/while/body/eval_jaxpr/reduce_scatter | solution.py:361
  2841.1 39.9 %all-reduce.3 = (f32[1,768]{1,0:T(1,128)S(1)}, f32[1,768]{1,0:T(1,128)S(1)}, f32[1,384]{1,0:T(1,128)S(1)}, f32[1,384]{1,0:T(1,128)S(1)}, f32[1,384]{1,0:T(1,128)S(1)}) all-reduce(f32[1,768]{1,0:T(1,128)S(1)} %get-tuple-element.1611, ...), channel_id=1, replica_groups=mesh['section'=2,'batch'=4,'mp'=4] {'section','batch','mp'}, use_global_device_ids=true, to_apply=%region_74.74 | all-reduce | flops 2688 | bytes 21504 | tf_op jit(solution)/shard_map/while/body/eval_jaxpr/psum | solution.py:368
  2882.7 104.5 %all-reduce.6.cloned.1.call-done = f32[1,768,384]{2,1,0:T(8,128)} async-done(((f32[1,768,384]{2,1,0:T(8,128)}), f32[1,768,384]{2,1,0:T(8,128)}) %all-reduce.6.cloned.1.call-update) | async-done | bytes 1179664 | tf_op jit(solution)/shard_map/while/body/eval_jaxpr/psum | solution.py:368
  2989.6 31.5 reduce-scatter.57.cloned.1.call-done
  3022.6 32.1 reduce-scatter.63.cloned.1.call-done
  3055.8 34.2 reduce-scatter.51.cloned.1.call-done
  3090.9 32.8 reduce-scatter.61.cloned.1.call-done
  3126.6 52.3 %reduce-scatter.49.cloned.1.call-done = f32[3,96,192]{2,1,0:T(8,128)} async-done(((f32[3,768,192]{2,1,0:T(8,128)}), f32[3,96,192]{2,1,0:T(8,128)}) %reduce-scatter.49.cloned.1.call-update) | async-done | bytes 221200 | tf_op jit(solution)/shard_map/while/body/eval_jaxpr/reduce_scatter | solution.py:359
  3180.5 53.9 %reduce-scatter.55.cloned.1.call-done = f32[96,768]{1,0:T(8,128)} async-done(((f32[768,768]{1,0:T(8,128)}), f32[96,768]{1,0:T(8,128)}) %reduce-scatter.55.cloned.1.call-update) | async-done | bytes 294928 | tf_op jit(solution)/shard_map/while
  3236.4 53.5 %reduce-scatter.53.cloned.1.call-done = f32[96,768]{1,0:T(8,128)} async-done(((f32[768,768]{1,0:T(8,128)}), f32[96,768]{1,0:T(8,128)}) %reduce-scatter.53.cloned.1.call-update) | async-done | bytes 294928 | tf_op jit(solution)/shard_map/while/body/eval_jaxpr/reduce_scatter | solution.py:361
  3315.0 39.9 %all-reduce.3 = (f32[1,768]{1,0:T(1,128)S(1)}, f32[1,768]{1,0:T(1,128)S(1)}, f32[1,384]{1,0:T(1,128)S(1)}, f32[1,384]{1,0:T(1,128)S(1)}, f32[1,384]{1,0:T(1,128)S(1)}) all-reduce(f32[1,768]{1,0:T(1,128)S(1)} %get-tuple-element.1611, ...), channel_id=1, replica_groups=mesh['section'=2,'batch'=4,'mp'=4] {'section','batch','mp'}, use_global_device_ids=true, to_apply=%region_74.74 | all-reduce | flops 2688 | bytes 21504 | tf_op jit(solution)/shard_map/while/body/eval_jaxpr/psum | solution.py:368
  3356.6 104.6 %all-reduce.6.cloned.1.call-done = f32[1,768,384]{2,1,0:T(8,128)} async-done(((f32[1,768,384]{2,1,0:T(8,128)}), f32[1,768,384]{2,1,0:T(8,128)}) %all-reduce.6.cloned.1.call-update) | async-done | bytes 1179664 | tf_op jit(solution)/shard_map/while/body/eval_jaxpr/psum | solution.py:368
  3463.7 31.9 reduce-scatter.57.cloned.1.call-done
  3497.0 32.1 reduce-scatter.63.cloned.1.call-done
  3530.1 34.1 reduce-scatter.51.cloned.1.call-done
  3565.2 32.6 reduce-scatter.61.cloned.1.call-done
  3600.7 52.5 %reduce-scatter.49.cloned.1.call-done = f32[3,96,192]{2,1,0:T(8,128)} async-done(((f32[3,768,192]{2,1,0:T(8,128)}), f32[3,96,192]{2,1,0:T(8,128)}) %reduce-scatter.49.cloned.1.call-update) | async-done | bytes 221200 | tf_op jit(solution)/shard_map/while/body/eval_jaxpr/reduce_scatter | solution.py:359
  3654.8 53.9 %reduce-scatter.55.cloned.1.call-done = f32[96,768]{1,0:T(8,128)} async-done(((f32[768,768]{1,0:T(8,128)}), f32[96,768]{1,0:T(8,128)}) %reduce-scatter.55.cloned.1.call-update) | async-done | bytes 294928 | tf_op jit(solution)/shard_map/while
  3710.7 53.7 %reduce-scatter.53.cloned.1.call-done = f32[96,768]{1,0:T(8,128)} async-done(((f32[768,768]{1,0:T(8,128)}), f32[96,768]{1,0:T(8,128)}) %reduce-scatter.53.cloned.1.call-update) | async-done | bytes 294928 | tf_op jit(solution)/shard_map/while/body/eval_jaxpr/reduce_scatter | solution.py:361
  (3046 shorter events, 1804.8 us)
Async XLA Ops:
  53.2 93.8 %reduce-scatter.45.cloned.1.call-start = ((), (), s32[]{:S(2)}) async-start(), calls=%async_computation.22 | async-start | bytes 368640 | tf_op jit(solution)/shard_map/while/body/eval_jaxpr/reduce_scatter | solution.py:63
  98.5 71.6 %reduce-scatter.35.cloned.1.call-start = ((), (), s32[]{:S(2)}) async-start(), calls=%async_computation.17 | async-start | bytes 491520 | tf_op jit(solution)/shard_map/while/body/eval_jaxpr/reduce_scatter | solution.py:53
  168.7 77.1 %reduce-scatter.39.cloned.1.call-start = ((), (), s32[]{:S(2)}) async-start(), calls=%async_computation.19 | async-start | bytes 491520 | tf_op jit(solution)/shard_map/while/body/eval_jaxpr/reduce_scatter | solution.py:63
  210.2 76.8 %reduce-scatter.41.cloned.1.call-start = ((), (), s32[]{:S(2)}) async-start(), calls=%async_computation.20 | async-start | bytes 491520 | tf_op jit(solution)/shard_map/while/body/eval_jaxpr/reduce_scatter | solution.py:53
  330.2 92.7 %reduce-scatter.45.cloned.1.call-start = ((), (), s32[]{:S(2)}) async-start(), calls=%async_computation.22 | async-start | bytes 368640 | tf_op jit(solution)/shard_map/while/body/eval_jaxpr/reduce_scatter | solution.py:63
  374.5 71.2 %reduce-scatter.35.cloned.1.call-start = ((), (), s32[]{:S(2)}) async-start(), calls=%async_computation.17 | async-start | bytes 491520 | tf_op jit(solution)/shard_map/while/body/eval_jaxpr/reduce_scatter | solution.py:53
  422.8 72.0 %reduce-scatter.47.cloned.1.call-start = ((), (), s32[]{:S(2)}) async-start(), calls=%async_computation.23 | async-start | bytes 368640 | tf_op jit(solution)/shard_map/while/body/eval_jaxpr/reduce_scatter | solution.py:63
  444.3 78.2 %reduce-scatter.39.cloned.1.call-start = ((), (), s32[]{:S(2)}) async-start(), calls=%async_computation.19 | async-start | bytes 491520 | tf_op jit(solution)/shard_map/while/body/eval_jaxpr/reduce_scatter | solution.py:63
  487.1 76.7 %reduce-scatter.41.cloned.1.call-start = ((), (), s32[]{:S(2)}) async-start(), calls=%async_computation.20 | async-start | bytes 491520 | tf_op jit(solution)/shard_map/while/body/eval_jaxpr/reduce_scatter | solution.py:53
  607.0 92.8 %reduce-scatter.45.cloned.1.call-start = ((), (), s32[]{:S(2)}) async-start(), calls=%async_computation.22 | async-start | bytes 368640 | tf_op jit(solution)/shard_map/while/body/eval_jaxpr/reduce_scatter | solution.py:63
  651.4 71.1 %reduce-scatter.35.cloned.1.call-start = ((), (), s32[]{:S(2)}) async-start(), calls=%async_computation.17 | async-start | bytes 491520 | tf_op jit(solution)/shard_map/while/body/eval_jaxpr/reduce_scatter | solution.py:53
  699.7 72.0 %reduce-scatter.47.cloned.1.call-start = ((), (), s32[]{:S(2)}) async-start(), calls=%async_computation.23 | async-start | bytes 368640 | tf_op jit(solution)/shard_map/while/body/eval_jaxpr/reduce_scatter | solution.py:63
  721.2 78.3 %reduce-scatter.39.cloned.1.call-start = ((), (), s32[]{:S(2)}) async-start(), calls=%async_computation.19 | async-start | bytes 491520 | tf_op jit(solution)/shard_map/while/body/eval_jaxpr/reduce_scatter | solution.py:63
  763.9 76.8 %reduce-scatter.41.cloned.1.call-start = ((), (), s32[]{:S(2)}) async-start(), calls=%async_computation.20 | async-start | bytes 491520 | tf_op jit(solution)/shard_map/while/body/eval_jaxpr/reduce_scatter | solution.py:53
  883.9 93.4 %reduce-scatter.45.cloned.1.call-start = ((), (), s32[]{:S(2)}) async-start(), calls=%async_computation.22 | async-start | bytes 368640 | tf_op jit(solution)/shard_map/while/body/eval_jaxpr/reduce_scatter | solution.py:63
  928.5 71.9 %reduce-scatter.35.cloned.1.call-start = ((), (), s32[]{:S(2)}) async-start(), calls=%async_computation.17 | async-start | bytes 491520 | tf_op jit(solution)/shard_map/while/body/eval_jaxpr/reduce_scatter | solution.py:53
  977.3 72.4 %reduce-scatter.47.cloned.1.call-start = ((), (), s32[]{:S(2)}) async-start(), calls=%async_computation.23 | async-start | bytes 368640 | tf_op jit(solution)/shard_map/while/body/eval_jaxpr/reduce_scatter | solution.py:63
  999.0 78.4 %reduce-scatter.39.cloned.1.call-start = ((), (), s32[]{:S(2)}) async-start(), calls=%async_computation.19 | async-start | bytes 491520 | tf_op jit(solution)/shard_map/while/body/eval_jaxpr/reduce_scatter | solution.py:63
  1042.0 76.8 %reduce-scatter.41.cloned.1.call-start = ((), (), s32[]{:S(2)}) async-start(), calls=%async_computation.20 | async-start | bytes 491520 | tf_op jit(solution)/shard_map/while/body/eval_jaxpr/reduce_scatter | solution.py:53
  1161.9 92.8 %reduce-scatter.45.cloned.1.call-start = ((), (), s32[]{:S(2)}) async-start(), calls=%async_computation.22 | async-start | bytes 368640 | tf_op jit(solution)/shard_map/while/body/eval_jaxpr/reduce_scatter | solution.py:63
  1206.2 71.4 %reduce-scatter.35.cloned.1.call-start = ((), (), s32[]{:S(2)}) async-start(), calls=%async_computation.17 | async-start | bytes 491520 | tf_op jit(solution)/shard_map/while/body/eval_jaxpr/reduce_scatter | solution.py:53
  1254.7 72.0 %reduce-scatter.47.cloned.1.call-start = ((), (), s32[]{:S(2)}) async-start(), calls=%async_computation.23 | async-start | bytes 368640 | tf_op jit(solution)/shard_map/while/body/eval_jaxpr/reduce_scatter | solution.py:63
  1276.2 78.2 %reduce-scatter.39.cloned.1.call-start = ((), (), s32[]{:S(2)}) async-start(), calls=%async_computation.19 | async-start | bytes 491520 | tf_op jit(solution)/shard_map/while/body/eval_jaxpr/reduce_scatter | solution.py:63
  1319.0 76.7 %reduce-scatter.41.cloned.1.call-start = ((), (), s32[]{:S(2)}) async-start(), calls=%async_computation.20 | async-start | bytes 491520 | tf_op jit(solution)/shard_map/while/body/eval_jaxpr/reduce_scatter | solution.py:53
  1438.8 92.8 %reduce-scatter.45.cloned.1.call-start = ((), (), s32[]{:S(2)}) async-start(), calls=%async_computation.22 | async-start | bytes 368640 | tf_op jit(solution)/shard_map/while/body/eval_jaxpr/reduce_scatter | solution.py:63
  1483.3 71.2 %reduce-scatter.35.cloned.1.call-start = ((), (), s32[]{:S(2)}) async-start(), calls=%async_computation.17 | async-start | bytes 491520 | tf_op jit(solution)/shard_map/while/body/eval_jaxpr/reduce_scatter | solution.py:53
  1531.6 71.7 %reduce-scatter.47.cloned.1.call-start = ((), (), s32[]{:S(2)}) async-start(), calls=%async_computation.23 | async-start | bytes 368640 | tf_op jit(solution)/shard_map/while/body/eval_jaxpr/reduce_scatter | solution.py:63
  1553.1 77.9 %reduce-scatter.39.cloned.1.call-start = ((), (), s32[]{:S(2)}) async-start(), calls=%async_computation.19 | async-start | bytes 491520 | tf_op jit(solution)/shard_map/while/body/eval_jaxpr/reduce_scatter | solution.py:63
  1595.6 76.6 %reduce-scatter.41.cloned.1.call-start = ((), (), s32[]{:S(2)}) async-start(), calls=%async_computation.20 | async-start | bytes 491520 | tf_op jit(solution)/shard_map/while/body/eval_jaxpr/reduce_scatter | solution.py:53
  1715.3 92.6 %reduce-scatter.45.cloned.1.call-start = ((), (), s32[]{:S(2)}) async-start(), calls=%async_computation.22 | async-start | bytes 368640 | tf_op jit(solution)/shard_map/while/body/eval_jaxpr/reduce_scatter | solution.py:63
  1759.7 71.1 %reduce-scatter.35.cloned.1.call-start = ((), (), s32[]{:S(2)}) async-start(), calls=%async_computation.17 | async-start | bytes 491520 | tf_op jit(solution)/shard_map/while/body/eval_jaxpr/reduce_scatter | solution.py:53
  1807.9 71.9 %reduce-scatter.47.cloned.1.call-start = ((), (), s32[]{:S(2)}) async-start(), calls=%async_computation.23 | async-start | bytes 368640 | tf_op jit(solution)/shard_map/while/body/eval_jaxpr/reduce_scatter | solution.py:63
  1829.4 78.1 %reduce-scatter.39.cloned.1.call-start = ((), (), s32[]{:S(2)}) async-start(), calls=%async_computation.19 | async-start | bytes 491520 | tf_op jit(solution)/shard_map/while/body/eval_jaxpr/reduce_scatter | solution.py:63
  1872.0 76.7 %reduce-scatter.41.cloned.1.call-start = ((), (), s32[]{:S(2)}) async-start(), calls=%async_computation.20 | async-start | bytes 491520 | tf_op jit(solution)/shard_map/while/body/eval_jaxpr/reduce_scatter | solution.py:53
  1991.9 93.2 %reduce-scatter.45.cloned.1.call-start = ((), (), s32[]{:S(2)}) async-start(), calls=%async_computation.22 | async-start | bytes 368640 | tf_op jit(solution)/shard_map/while/body/eval_jaxpr/reduce_scatter | solution.py:63
  2036.4 71.8 %reduce-scatter.35.cloned.1.call-start = ((), (), s32[]{:S(2)}) async-start(), calls=%async_computation.17 | async-start | bytes 491520 | tf_op jit(solution)/shard_map/while/body/eval_jaxpr/reduce_scatter | solution.py:53
  2085.1 71.8 %reduce-scatter.47.cloned.1.call-start = ((), (), s32[]{:S(2)}) async-start(), calls=%async_computation.23 | async-start | bytes 368640 | tf_op jit(solution)/shard_map/while/body/eval_jaxpr/reduce_scatter | solution.py:63
  2106.8 77.8 %reduce-scatter.39.cloned.1.call-start = ((), (), s32[]{:S(2)}) async-start(), calls=%async_computation.19 | async-start | bytes 491520 | tf_op jit(solution)/shard_map/while/body/eval_jaxpr/reduce_scatter | solution.py:63
  2149.1 76.7 %reduce-scatter.41.cloned.1.call-start = ((), (), s32[]{:S(2)}) async-start(), calls=%async_computation.20 | async-start | bytes 491520 | tf_op jit(solution)/shard_map/while/body/eval_jaxpr/reduce_scatter | solution.py:53
  2240.2 1539.7 %collective-permute-start.2 = (bf16[3,64,768]{2,1,0:T(8,128)(2,1)}, bf16[3,64,768]{2,1,0:T(8,128)(2,1)}, u32[]{:S(2)}, u32[]{:S(2)}) collective-permute-start(bf16[3,64,768]{2,1,0:T(8,128)(2,1)} %slice.168), channel_id=1, source_target_pairs={{0,16},{1,17},{2,18},{3,19},{4,20},{5,21},{6,22},{7,23},{8,24},{9,... | collective-permute-start | bytes 884744 | tf_op jit(solution)/shard_map/ppermute | solution.py:23
  2343.9 169.8 %all-reduce.6.cloned.1.call-start = ((), (), s32[]{:S(2)}) async-start(), calls=%async_computation.32 | async-start | bytes 2359296 | tf_op jit(solution)/shard_map/while/body/eval_jaxpr/psum | solution.py:368
  2346.7 200.8 %reduce-scatter.57.cloned.1.call-start = ((), (), s32[]{:S(2)}) async-start(), calls=%async_computation.28 | async-start | bytes 663552 | tf_op jit(solution)/shard_map/while/body/eval_jaxpr/reduce_scatter | solution.py:363
  2348.9 232.2 %reduce-scatter.63.cloned.1.call-start = ((), (), s32[]{:S(2)}) async-start(), calls=%async_computation.31 | async-start | bytes 663552 | tf_op jit(solution)/shard_map/while
  2351.1 265.2 %reduce-scatter.51.cloned.1.call-start = ((), (), s32[]{:S(2)}) async-start(), calls=%async_computation.25 | async-start | bytes 884736 | tf_op jit(solution)/shard_map/while
  2353.5 296.4 %reduce-scatter.61.cloned.1.call-start = ((), (), s32[]{:S(2)}) async-start(), calls=%async_computation.30 | async-start | bytes 663552 | tf_op jit(solution)/shard_map/while/body/eval_jaxpr/reduce_scatter | solution.py:365
  2355.5 349.6 %reduce-scatter.49.cloned.1.call-start = ((), (), s32[]{:S(2)}) async-start(), calls=%async_computation.24 | async-start | bytes 2654208 | tf_op jit(solution)/shard_map/while/body/eval_jaxpr/reduce_scatter | solution.py:359
  2359.1 401.5 %reduce-scatter.55.cloned.1.call-start = ((), (), s32[]{:S(2)}) async-start(), calls=%async_computation.27 | async-start | bytes 2654208 | tf_op jit(solution)/shard_map/while
  2363.0 453.0 %reduce-scatter.53.cloned.1.call-start = ((), (), s32[]{:S(2)}) async-start(), calls=%async_computation.26 | async-start | bytes 2654208 | tf_op jit(solution)/shard_map/while/body/eval_jaxpr/reduce_scatter | solution.py:361
  2818.6 168.7 %all-reduce.6.cloned.1.call-start = ((), (), s32[]{:S(2)}) async-start(), calls=%async_computation.32 | async-start | bytes 2359296 | tf_op jit(solution)/shard_map/while/body/eval_jaxpr/psum | solution.py:368
  2821.4 199.7 %reduce-scatter.57.cloned.1.call-start = ((), (), s32[]{:S(2)}) async-start(), calls=%async_computation.28 | async-start | bytes 663552 | tf_op jit(solution)/shard_map/while/body/eval_jaxpr/reduce_scatter | solution.py:363
  2823.6 231.1 %reduce-scatter.63.cloned.1.call-start = ((), (), s32[]{:S(2)}) async-start(), calls=%async_computation.31 | async-start | bytes 663552 | tf_op jit(solution)/shard_map/while
  2825.9 264.1 %reduce-scatter.51.cloned.1.call-start = ((), (), s32[]{:S(2)}) async-start(), calls=%async_computation.25 | async-start | bytes 884736 | tf_op jit(solution)/shard_map/while
  2828.2 295.5 %reduce-scatter.61.cloned.1.call-start = ((), (), s32[]{:S(2)}) async-start(), calls=%async_computation.30 | async-start | bytes 663552 | tf_op jit(solution)/shard_map/while/body/eval_jaxpr/reduce_scatter | solution.py:365
  2830.2 348.6 %reduce-scatter.49.cloned.1.call-start = ((), (), s32[]{:S(2)}) async-start(), calls=%async_computation.24 | async-start | bytes 2654208 | tf_op jit(solution)/shard_map/while/body/eval_jaxpr/reduce_scatter | solution.py:359
  2833.8 400.6 %reduce-scatter.55.cloned.1.call-start = ((), (), s32[]{:S(2)}) async-start(), calls=%async_computation.27 | async-start | bytes 2654208 | tf_op jit(solution)/shard_map/while
  2837.7 452.2 %reduce-scatter.53.cloned.1.call-start = ((), (), s32[]{:S(2)}) async-start(), calls=%async_computation.26 | async-start | bytes 2654208 | tf_op jit(solution)/shard_map/while/body/eval_jaxpr/reduce_scatter | solution.py:361
  3292.5 168.8 %all-reduce.6.cloned.1.call-start = ((), (), s32[]{:S(2)}) async-start(), calls=%async_computation.32 | async-start | bytes 2359296 | tf_op jit(solution)/shard_map/while/body/eval_jaxpr/psum | solution.py:368
  3295.3 200.2 %reduce-scatter.57.cloned.1.call-start = ((), (), s32[]{:S(2)}) async-start(), calls=%async_computation.28 | async-start | bytes 663552 | tf_op jit(solution)/shard_map/while/body/eval_jaxpr/reduce_scatter | solution.py:363
  3297.5 231.6 %reduce-scatter.63.cloned.1.call-start = ((), (), s32[]{:S(2)}) async-start(), calls=%async_computation.31 | async-start | bytes 663552 | tf_op jit(solution)/shard_map/while
  3299.7 264.5 %reduce-scatter.51.cloned.1.call-start = ((), (), s32[]{:S(2)}) async-start(), calls=%async_computation.25 | async-start | bytes 884736 | tf_op jit(solution)/shard_map/while
  3302.1 295.7 %reduce-scatter.61.cloned.1.call-start = ((), (), s32[]{:S(2)}) async-start(), calls=%async_computation.30 | async-start | bytes 663552 | tf_op jit(solution)/shard_map/while/body/eval_jaxpr/reduce_scatter | solution.py:365
  3304.1 349.0 %reduce-scatter.49.cloned.1.call-start = ((), (), s32[]{:S(2)}) async-start(), calls=%async_computation.24 | async-start | bytes 2654208 | tf_op jit(solution)/shard_map/while/body/eval_jaxpr/reduce_scatter | solution.py:359
  3307.7 401.0 %reduce-scatter.55.cloned.1.call-start = ((), (), s32[]{:S(2)}) async-start(), calls=%async_computation.27 | async-start | bytes 2654208 | tf_op jit(solution)/shard_map/while
  3311.6 452.8 %reduce-scatter.53.cloned.1.call-start = ((), (), s32[]{:S(2)}) async-start(), calls=%async_computation.26 | async-start | bytes 2654208 | tf_op jit(solution)/shard_map/while/body/eval_jaxpr/reduce_scatter | solution.py:361
  (744 other events, 10341.8 us)
Sparse Core Ops, SparseCore 0:
  37.1 24.4 reduce-scatter.42
  64.4 24.5 reduce-scatter.32
  221.3 24.4 reduce-scatter.38
  341.6 24.7 reduce-scatter.32
  374.6 24.4 reduce-scatter.44
  415.4 24.7 reduce-scatter.34
  442.9 24.4 reduce-scatter.36
  498.0 24.4 reduce-scatter.38
  539.3 24.4 reduce-scatter.40
  591.3 24.4 reduce-scatter.42
  618.5 24.7 reduce-scatter.32
  692.2 24.4 reduce-scatter.34
  719.6 24.4 reduce-scatter.36
  775.0 24.4 reduce-scatter.38
  816.3 24.4 reduce-scatter.40
  895.3 24.5 reduce-scatter.32
  928.7 24.9 reduce-scatter.44
  969.9 24.9 reduce-scatter.34
  997.8 24.4 reduce-scatter.36
  1094.3 24.4 reduce-scatter.40
  1173.4 24.7 reduce-scatter.32
  1206.3 24.6 reduce-scatter.44
  1247.2 24.7 reduce-scatter.34
  1274.7 24.4 reduce-scatter.36
  1329.9 24.4 reduce-scatter.38
  1423.2 24.4 reduce-scatter.42
  1450.4 24.8 reduce-scatter.32
  1483.4 24.4 reduce-scatter.44
  1524.2 24.4 reduce-scatter.34
  1551.4 24.4 reduce-scatter.36
  1606.5 24.4 reduce-scatter.38
  1726.9 24.7 reduce-scatter.32
  1759.8 24.4 reduce-scatter.44
  1800.6 24.4 reduce-scatter.34
  2003.3 24.7 reduce-scatter.32
  2036.5 24.4 reduce-scatter.44
  2104.8 24.4 reduce-scatter.36
  2346.7 31.1 reduce-scatter.58
  2383.8 129.8 all-reduce.5
  2515.8 31.6 reduce-scatter.56
  2549.8 31.2 reduce-scatter.62
  2583.4 32.8 reduce-scatter.50
  2618.4 31.4 reduce-scatter.60
  2652.2 52.8 reduce-scatter.48
  2707.4 53.1 reduce-scatter.54
  2762.8 53.1 reduce-scatter.52
  2821.2 30.2 reduce-scatter.58
  2857.4 129.7 all-reduce.5
  2989.5 31.6 reduce-scatter.56
  3023.4 31.2 reduce-scatter.62
  3057.0 32.8 reduce-scatter.50
  3092.2 31.4 reduce-scatter.60
  3126.1 52.7 reduce-scatter.48
  3181.3 53.1 reduce-scatter.54
  3236.7 53.1 reduce-scatter.52
  3295.3 30.2 reduce-scatter.58
  3331.5 129.6 all-reduce.5
  3463.6 31.8 reduce-scatter.56
  3497.7 31.4 reduce-scatter.62
  3531.2 32.9 reduce-scatter.50
  3566.3 31.4 reduce-scatter.60
  3600.1 52.9 reduce-scatter.48
  3655.5 53.1 reduce-scatter.54
  3711.2 53.1 reduce-scatter.52
  (27 shorter events, 654.1 us)
where the time goes:
time: 3810 us; the launch traced here: 3790 us
  waiting for transfers between devices  1750 us (46%)
  blocking collectives  893 us (23%)
  matrix products  479 us (13%)
  local copies, waits for them, and re-layouts  332 us (9%)
  other arithmetic  257 us (7%)
    all_gather x48, blocking collectives, spread_rows(): return lax.all_gather(values, 'mp', axis=0, tiled=True)  466 us
    reduce_scatter x32, waiting for transfers between devices, collect_grads(): lax.psum_scatter(values.astype(jnp.bfloat16), 'mp', scatter_dimension=0,...  421 us
    while x103, waiting for transfers between devices  362 us
    psum x3, waiting for transfers between devices, reduce_step(): minor_part = lax.psum(minor_item, ('section', 'batch', 'mp'))  315 us
    all_gather x32, blocking collectives, spread_grads(): return lax.all_gather(values, 'mp', axis=0, tiled=True)  307 us
    reduce_scatter x3, waiting for transfers between devices, reduce_step(): lax.psum_scatter(large_item[2], ('section', 'batch'), scatter_dimension=0...  161 us
    reduce_scatter x3, waiting for transfers between devices, reduce_step(): lax.psum_scatter(large_item[0], ('section', 'batch'), scatter_dimension=1...  157 us
    reduce_scatter x32, waiting for transfers between devices, collect_rows(): lax.psum_scatter(values.astype(jnp.bfloat16), 'mp', scatter_dimension=0,...  139 us
  transfers between devices with their start and end apart: 108, of which 56 were waited for; matrix products, arithmetic and copies ran while one was open for 23% of the time, Pallas kernels for 0%

commit v1 on v0

v1 whole, which is shorter than its diff:
```python
import functools
import math

import jax
import jax.numpy as jnp
from jax import lax
from jax.experimental import pallas as pl
from jax.experimental.pallas import tpu as pltpu
from jax.sharding import PartitionSpec as P

HEADS = 12
PHEADS = 12
CAP_C = 256
CAP_T = 128
IMGS = 4
EPS = 1e-6
LOG2E = math.log2(math.e)
MESH = pl.DeviceIdType.MESH
F32 = jnp.float32
BF16 = jnp.bfloat16

(
    AG_H1, RS_O, AG_H2, RS_A, AG_P1, RS_PO, AG_P2, AG_COT, RS_P2, AG_PB, RS_P1,
    AG_DY, RS_2, AG_B, RS_1, AG_PIN,
) = range(16)
N_PHASE = 16
DIRECT = (8, 9)
Z_FIRST = (2, 8)
N_ACT = 56


def mm(a, b):
    return lax.dot_general(a, b, (((1,), (0,)), ((), ())), preferred_element_type=F32)


def mm_nt(a, b):
    return lax.dot_general(a, b, (((1,), (1,)), ((), ())), preferred_element_type=F32)


def mm_tn(a, b):
    return lax.dot_general(a, b, (((0,), (0,)), ((), ())), preferred_element_type=F32)


def mean_of(x):
    return jnp.sum(x, axis=-1, keepdims=True) * (1.0 / x.shape[-1])


def norm_parts(x):
    cen = x - mean_of(x)
    rstd = lax.rsqrt(mean_of(cen * cen) + EPS)
    return cen * rstd, rstd


def norm_forward(x, gain):
    return norm_parts(x)[0] * gain


def norm_backward(x, gain, dh):
    xhat, rstd = norm_parts(x)
    dxh = dh * gain
    dx = rstd * (dxh - mean_of(dxh) - xhat * mean_of(dxh * xhat))
    return dx, dh * xhat


def fold(values):
    total = values[0:8]
    for top in range(8, values.shape[0], 8):
        total = total + values[top:top + 8]
    return total


def reciprocal(x):
    guess = pl.reciprocal(x, approx=True)
    return guess * (2.0 - x * guess)


def turns(angle):
    quarter = jnp.floor(angle * (2.0 / math.pi) + 0.5)
    rest = (angle - quarter * 1.5703125) - quarter * (math.pi / 2 - 1.5703125)
    sq = rest * rest
    sine = rest + rest * sq * (
        -1.0 / 6 + sq * (1.0 / 120 + sq * (-1.0 / 5040 + sq * (1.0 / 362880)))
    )
    cosine = 1.0 + sq * (
        -0.5 + sq * (1.0 / 24 + sq * (-1.0 / 720 + sq * (1.0 / 40320 - sq * (1.0 / 3628800))))
    )
    turn = quarter - 4.0 * jnp.floor(quarter * 0.25)
    odd = jnp.logical_or(turn == 1.0, turn == 3.0)
    first = jnp.where(odd, cosine, sine)
    second = jnp.where(odd, sine, cosine)
    return (
        jnp.where(turn >= 2.0, -first, first),
        jnp.where(jnp.logical_or(turn == 1.0, turn == 2.0), -second, second),
    )


ERF = (0.254829592, -0.284496736, 1.421413741, -1.453152027, 1.061405429)
ERF_P = 0.3275911


def gelu_parts(u):
    bell = jnp.exp(u * u * -0.5)
    below = 1.0 + jnp.abs(u) * (ERF_P * math.sqrt(0.5))
    w = reciprocal(below)
    poly = 0.5 * ERF[4]
    for coefficient in ERF[3::-1]:
        poly = poly * w + 0.5 * coefficient
    tail = poly * w * bell
    phi = jnp.where(u >= 0.0, 1.0 - tail, tail)
    return u * phi, phi + u * bell * (1.0 / math.sqrt(2.0 * math.pi))


def head_mask(width, size, head):
    lane = lax.broadcasted_iota(jnp.int32, (1, width), 1)
    inside = jnp.logical_and(lane >= head * size, lane < (head + 1) * size)
    return jnp.where(inside, 1.0, 0.0).astype(BF16)


def segment(place, bounds):
    place = place.astype(F32)
    total = jnp.zeros(place.shape, F32)
    for bound in bounds:
        total = total + jnp.where(place >= bound, 1.0, 0.0)
    return total


def bounds_of(ref, row):
    lengths = ref[0].astype(F32)
    lane = lax.broadcasted_iota(jnp.int32, lengths.shape, 1)
    own = jnp.sum(jnp.where(lane == row, lengths, 0.0), axis=1, keepdims=True)
    ends = []
    total = jnp.zeros((1, 1), F32)
    for i in range(IMGS):
        total = total + own[i:i + 1, :]
        ends.append(total)
    return ends


def mega(
    nb, z_inside,
    ctx_len, tgt_len, places, x_ref, cot_ref, gain_e1, gain_e2, mask_token, gain_p1, gain_p2,
    *rest,
):
    n_weight = 9
    n_out = 8
    n_grad = 9
    n_minor = 5
    w_hbm = rest[:n_weight]
    rest = rest[n_weight:]
    dx_out = rest[0]
    grad_out = rest[1:1 + n_out]
    l_all = rest[1 + n_out]
    minor_out = rest[2 + n_out:2 + n_out + n_minor]
    rest = rest[2 + n_out + n_minor:]
    w_vmem = rest[:n_weight]
    eqkv, eproj, eup, edown, link, pqkv, pproj, pup, pdown = w_vmem
    w_sem, wys, wyr, wzs, wzr, wcs, wcr = rest[n_weight:n_weight + 7]
    rest = rest[n_weight + 7:]
    (
        xin, cin, pin, h1g, q_s, kv_s, o_s, p_a, p_b, part, rb_o, x1_s, h2g, a_s, gp_s, rb_a,
        y_s, z_s, ph1g, pt1, pq_s, pkv_s, po_s, pp_a, pp_b, part_p, rb_po, m_s, px1_s, ph2g,
        pa_s, cotg, pdu_s, rb_p2, pdbg, pdq_s, pdkv_s, pdkv_acc, pdkv_x, pdkv_r,
        part_p1, rb_p1, dcg, dyg, rb_2, dx1_s, dbg, dqkv_s, dkv_acc, dkv_x, dkv_r,
        rb_1, dx_s, dx_r, ds_s, pds_s,
    ) = rest[:N_ACT]
    rest = rest[N_ACT:]
    g_full = rest[0:n_grad]
    g_core = rest[n_grad:2 * n_grad]
    g_y = rest[2 * n_grad:3 * n_grad]
    g_z = rest[3 * n_grad:4 * n_grad]
    (
        l_full, l_core, l_half, l_mp, l_z,
        minor, m_core, m_mp, m_z,
        ss, rs, ins, inr, inl, kvs, kvr, dxs, dxr,
        gcs, gcr, gys, gyr, gzs, gzr, lcs, lcr, lms, lmr, lzs, lzr, las, lar,
        mcs, mcr, mms, mmr, mzs, mzr,
    ) = rest[4 * n_grad:]

    n_mp = 4
    r = lax.axis_index("mp")
    s = lax.axis_index("section")
    z = lax.axis_index("batch")
    x = lax.rem(r, 2)
    y = lax.div(r, 2)
    x_peer = r + 1 - 2 * x
    y_peer = r + 2 - 4 * y
    other = 1 - s
    pair = lax.rem(z, 2)
    z_pair = z + 1 - 2 * pair
    nm = h1g.shape[0]
    base = y * nm
    W = x_ref.shape[-1]
    PW = cot_ref.shape[-1]
    HC = x_ref.shape[2]
    HT = cot_ref.shape[2]
    HB = HC + HT
    heads = HEADS // n_mp
    pheads = PHEADS // n_mp
    wq = q_s.shape[-1]
    wpq = pq_s.shape[-1]
    FH = a_s.shape[-1]
    PF = pa_s.shape[-1]
    scale = (wq // heads) ** -0.5
    pscale = (wpq // pheads) ** -0.5
    en1, en2, pn1, pn2 = (
        ref[...].reshape(1, ref.shape[0]) for ref in (gain_e1, gain_e2, gain_p1, gain_p2)
    )

    def mp_peer(j):
        return lax.rem(r + j, n_mp)

    def mp_source(j):
        return lax.rem(r + n_mp - j, n_mp)

    def z_peer(j):
        return lax.rem(z + j, nb)

    def z_source(j):
        return lax.rem(z + nb - j, nb)

    def rows_at(block, rows):
        return pl.ds(pl.multiple_of(block * rows, rows), rows)

    def send_to(src, dst, send_sem, recv_sem, **device):
        return pltpu.make_async_remote_copy(
            src_ref=src, dst_ref=dst, send_sem=send_sem, recv_sem=recv_sem,
            device_id=device, device_id_type=MESH,
        )

    def landing(chunk):
        return xin.at[chunk], cin.at[chunk], pin.at[chunk, x]

    def local_copies(part, mb):
        chunk = y if part == 0 else 2
        sources = (x_ref.at[0, mb], cot_ref.at[0, mb], places.at[mb])
        return [
            pltpu.make_async_copy(src, dst, inl.at[part, n])
            for n, (src, dst) in enumerate(zip(sources, landing(chunk)))
        ]

    for copy in local_copies(0, base + s):
        copy.start()

    @pl.when(s == y)
    def _():
        for copy in local_copies(1, base + 2):
            copy.start()

    def own_quarter(i):
        dst = w_vmem[i] if i == 4 else w_vmem[i].at[0]
        return pltpu.make_async_copy(w_hbm[i], dst, w_sem.at[i])

    for i in range(n_weight):
        own_quarter(i).start()

    barrier = pltpu.get_barrier_semaphore()
    for j in range(1, n_mp):
        pl.semaphore_signal(barrier, inc=1, device_id={"mp": mp_peer(j)}, device_id_type=MESH)
    for j in range(1, nb):
        pl.semaphore_signal(barrier, inc=1, device_id={"batch": z_peer(j)}, device_id_type=MESH)
    pl.semaphore_signal(barrier, inc=1, device_id={"section": other}, device_id_type=MESH)
    pl.semaphore_signal(
        barrier, inc=1, device_id={"section": other, "mp": y_peer}, device_id_type=MESH
    )
    pl.semaphore_wait(barrier, n_mp - 1 + nb - 1 + 2)

    def input_copies(part, mb):
        chunk = y if part == 0 else 2
        sources = (x_ref.at[0, mb], cot_ref.at[0, mb], places.at[mb])
        return [
            send_to(src, dst, ins.at[part, n], inr.at[part, n], mp=y_peer)
            for n, (src, dst) in enumerate(zip(sources, landing(chunk)))
        ]

    def input_waits(part):
        chunk = 1 - y if part == 0 else 2
        for n, dst in enumerate(landing(chunk)):
            send_to(dst, dst, ins.at[part, n], inr.at[part, n], mp=y_peer).wait_recv()

    far = (1 - y) * nm
    for copy in input_copies(0, far + s):
        copy.start()

    @pl.when(s == y)
    def _():
        for copy in input_copies(1, far + 2):
            copy.start()

    n_parcel = 12

    def parcel(refs, n):
        if n < 3:
            return refs[0].at[n]
        if n == 3:
            return refs[1]
        if n < 8:
            ref = refs[2 + (n - 4) // 2]
            rows = ref.shape[0] // 2
            return ref.at[pl.ds((n - 4) % 2 * rows, rows)]
        return refs[n - 3]

    def share(n, ref, number, of):
        if n == 8:
            rows = ref.shape[1] // of
            return ref.at[:, rows_at(number, rows)]
        rows = ref.shape[0] // of
        return ref.at[rows_at(number, rows)]

    away = [ref if i == 4 else ref.at[1] for i, ref in enumerate(w_vmem)]

    def p_far(n):
        number, of = (s, 2) if n in DIRECT else (2 * s + pair, 4)
        return send_to(
            share(n, parcel(w_hbm, n), number, of), share(n, parcel(away, n), number, of),
            wys.at[n], wyr.at[n], mp=y_peer,
        )

    def p_pair(n, which):
        block = share(n, parcel(away, n), 2 * s + which, 4)
        return send_to(block, block, wzs.at[n], wzr.at[n], batch=z_pair)

    def p_swap(n, which):
        block = share(n, parcel(away, n), which, 2)
        return send_to(block, block, wcs.at[n], wcr.at[n], section=other)

    def fetch(*parcels):
        for n in parcels:
            p_far(n).start()

    def to_pair(*parcels):
        for n in parcels:
            p_far(n).wait_recv()
            p_pair(n, pair).start()

    def to_core(*parcels):
        for n in parcels:
            if n not in DIRECT:
                p_pair(n, 1 - pair).wait_recv()
            else:
                p_far(n).wait_recv()
            p_swap(n, s).start()

    def arrived(*parcels):
        for n in parcels:
            p_swap(n, other).wait_recv()

    def at_hand(*matrices):
        for i in matrices:
            own_quarter(i).wait()

    fetch(0, 1, 2, 3)

    def ag_send(buf, rows, ph, c):
        mine = buf.at[c, rows_at(x, rows)]
        send_to(mine, mine, ss.at[ph, c], rs.at[ph, c], mp=x_peer).start()

    def ag_wait(buf, rows, ph, c):
        theirs = buf.at[c, rows_at(1 - x, rows)]
        send_to(theirs, theirs, ss.at[ph, c], rs.at[ph, c], mp=x_peer).wait_recv()

    def rs_copy(part, rb, rows, ph, c):
        return send_to(
            part.at[c, rows_at(1 - x, rows)], rb.at[c], ss.at[ph, c], rs.at[ph, c], mp=x_peer
        )

    def rs_send(part, rb, rows, ph, c):
        rs_copy(part, rb, rows, ph, c).start()

    def own_sum(part, rb, rows, c, top, size):
        at = pl.ds(pl.multiple_of(x * rows + top, 16), size)
        return part[c, at, :].astype(F32) + rb[c, top:top + size, :].astype(F32)

    def own_tile(rows, top, size):
        return pl.ds(pl.multiple_of(x * rows + top, 16), size)

    def ex_copy(src, dst, ph, c):
        return send_to(src.at[c], dst.at[c], ss.at[ph, c], rs.at[ph, c], mp=x_peer)

    def ex_wait(src, dst, ph, c):
        ex_copy(src, dst, ph, c).wait_recv()

    def ex_sum(src, dst, c, at):
        return src[c, at, :].astype(F32) + dst[c, at, :].astype(F32)

    def pin_copy(c, block):
        at = pin.at[c, block]
        return send_to(at, at, ss.at[AG_PIN, c], rs.at[AG_PIN, c], mp=x_peer)

    def each(body, first=0):
        def step(n, carry):
            body(lax.rem(n + first, nm) if first else n)
            return carry
        lax.fori_loop(0, nm, step, 0)

    def spot(c):
        return jnp.where(c == 2, s, c), base + jnp.where(c == 2, 2, s), lax.div(c, 2)

    def minor_add(row, values):
        width = values.shape[-1]
        values = jnp.sum(values, axis=0, keepdims=True)
        minor[pl.ds(row, 1), 0:width] = minor[pl.ds(row, 1), 0:width] + values

    def wgrad(lhs, rhs, chunk, *targets):
        rows = lhs.shape[0] * lhs.shape[1]

        def step(n, carry):
            at = pl.ds(pl.multiple_of(n * chunk, chunk), chunk)
            left = lhs[:, :, at].reshape(rows, chunk).T
            for i in range(2):
                for matrix, lead, first, last in targets:
                    right = rhs[i, :, :, first:last].reshape(rows, last - first)
                    g_full[matrix][i, at, lead:lead + last - first] = mm(left, right).astype(BF16)
            return carry
        lax.fori_loop(0, lhs.shape[-1] // chunk, step, 0)

    def pieces(rows, body):
        size = rows // 4

        def step(n, carry):
            body(n, size)
            return carry
        lax.fori_loop(0, 4, step, 0)

    def half_rows(i):
        return g_full[i].shape[1] // 2

    def core_copy(i):
        return send_to(
            g_full[i].at[:, rows_at(other, half_rows(i))], g_core[i], gcs.at[i], gcr.at[i],
            section=other,
        )

    def core_start(i):
        core_copy(i).start()

    def put(i, total, at=slice(None)):
        first = (0, 2, 3, 4, 6, 7, 0, 2, 3)[i]
        if i == 0:
            for part in range(2):
                grad_out[0][part, at, :] = total[:, part * wq:(part + 1) * wq]
        elif i == 6:
            grad_out[0][2, at, :] = total[:, 0:wq]
            tail = total[:, wq:]
            grad_out[1][at, :] = tail.T if z_inside else tail
        elif i == 3:
            for part in range(3):
                grad_out[4][part, at, :] = total[:, part * wpq:(part + 1) * wpq]
            grad_out[5][at, :] = total[:, 3 * wpq:]
        elif i in (1, 2):
            grad_out[first][at, 0:FH // 2] = total
        elif i in (7, 8):
            grad_out[first][at, FH // 2:FH] = total
        else:
            grad_out[first][at, :] = total

    z_far = lax.rem(z + 2, 4)

    def z_slice(i, number):
        rows = half_rows(i) // 4
        return pl.ds(pl.multiple_of(s * half_rows(i) + number * rows, rows), rows)

    def near_copies(i):
        return [
            send_to(
                g_full[i].at[j, z_slice(i, 1 - pair + 2 * m)], g_z[i].at[2 * j + m],
                gzs.at[i, 2 * j + m], gzr.at[i, 2 * j + m], batch=z_pair,
            )
            for j in ((1, 0) if i in Z_FIRST else (0,)) for m in range(2)
        ]

    def y_copies(i):
        if not z_inside or i not in Z_FIRST:
            mine = g_full[i].at[1, rows_at(s, half_rows(i))]
            return [send_to(mine, g_y[i].at[0], gys.at[i, 0], gyr.at[i, 0], mp=y_peer)]
        return [
            send_to(
                g_full[i].at[1, z_slice(i, pair + 2 * m)], g_y[i].at[m], gys.at[i, m],
                gyr.at[i, m], mp=y_peer,
            )
            for m in range(2)
        ]

    def far_copy(i):
        return send_to(
            g_full[i].at[0, z_slice(i, z_far)], g_z[i].at[4], gzs.at[i, 4], gzr.at[i, 4],
            batch=z_far,
        )

    def add_core(i):
        core_copy(i).wait_recv()

        def piece(n, size):
            mine, at = rows_at(4 * s + n, size), rows_at(n, size)
            for j in range(2):
                g_full[i][j, mine, :] = g_full[i][j, mine, :] + g_core[i][j, at, :]

        pieces(half_rows(i), piece)

    def add_near(i):
        for copy in near_copies(i):
            copy.wait_recv()
        for j in (1, 0) if i in Z_FIRST else (0,):
            for m in range(2):
                at = z_slice(i, pair + 2 * m)
                g_full[i][j, at, :] = g_full[i][j, at, :] + g_z[i][2 * j + m]

    def add_y(i):
        for copy in y_copies(i):
            copy.wait_recv()
        if i in Z_FIRST:
            for m in range(2):
                at = z_slice(i, pair + 2 * m)
                g_full[i][0, at, :] = g_full[i][0, at, :] + g_y[i][m]
            return

        def piece(n, size):
            mine, at = rows_at(4 * s + n, size), rows_at(n, size)
            g_full[i][0, mine, :] = g_full[i][0, mine, :] + g_y[i][0, at, :]

        pieces(half_rows(i), piece)

    def near(*matrices):
        for i in matrices:
            add_core(i)
            for copy in near_copies(i) if z_inside and i in Z_FIRST else y_copies(i):
                copy.start()

    def across(*matrices):
        if not z_inside:
            return
        for i in matrices:
            if i in Z_FIRST:
                add_near(i)
            else:
                add_y(i)
            for copy in y_copies(i) if i in Z_FIRST else near_copies(i):
                copy.start()

    def onward(*matrices):
        for i in matrices:
            if not z_inside:
                for copy in y_copies(i):
                    copy.wait_recv()
                put(i, g_full[i][0, rows_at(s, half_rows(i)), :] + g_y[i][0])
                continue
            if i in Z_FIRST:
                add_y(i)
            else:
                add_near(i)
            far_copy(i).start()

    def finish(*matrices):
        if not z_inside:
            return
        for i in matrices:
            far_copy(i).wait_recv()
            put(i, g_full[i][0, z_slice(i, z), :].astype(F32) + g_z[i][4].astype(F32))

    def first_rows(c):
        for top in range(0, HC, 16):
            rows = xin[c, top:top + 16, :].astype(F32)
            h1g[c, own_tile(HC, top, 16), :] = norm_forward(rows, en1).astype(BF16)
        ag_send(h1g, HC, AG_H1, c)
        cotg[c, rows_at(x, HT), :] = cin[c]
        ag_send(cotg, HT, AG_COT, c)
        pin_copy(c, x).start()

    for copy in local_copies(0, base + s):
        copy.wait()
    minor[...] = jnp.zeros_like(minor)

    def first_step(n, carry):
        @pl.when(n == 1)
        def _():
            input_waits(0)

        @pl.when(jnp.logical_and(n == 2, s != y))
        def _():
            input_waits(1)

        @pl.when(jnp.logical_and(n == 2, s == y))
        def _():
            for copy in local_copies(1, base + 2):
                copy.wait()

        first_rows(jnp.where(n == 2, 2, jnp.where(n == 0, y, 1 - y)))
        return carry

    lax.fori_loop(0, nm, first_step, 0)

    half = PW // 2
    frequency = jnp.exp(
        lax.broadcasted_iota(jnp.int32, (1, half), 1).astype(F32)
        * (-2.0 * math.log(10000.0) / PW)
    )

    def mask_rows(c):
        pin_copy(c, 1 - x).wait_recv()
        here = lax.broadcasted_iota(jnp.int32, (HT, HT), 0)
        there = lax.broadcasted_iota(jnp.int32, (HT, HT), 1)
        for b in range(2):
            row = pin[c, b].astype(F32)
            column = jnp.sum(jnp.where(here == there, row, 0.0), axis=1, keepdims=True)
            sine, cosine = turns(column * frequency)
            at = slice(b * HT, (b + 1) * HT)
            m_s[c, at, 0:half] = sine
            m_s[c, at, half:PW] = cosine
        for b in range(2):
            at = slice(b * HT, (b + 1) * HT)
            rows = m_s[c, at, :] + mask_token[...].reshape(1, PW)
            m_s[c, at, :] = rows
            normed = norm_forward(rows, pn1).astype(BF16)
            pt1[c, at, :] = normed
            ph1g[c, b * HB + HC:(b + 1) * HB, :] = normed

    n_row = 2 * HC
    n_ctx = n_mp * HC

    def kv_copy(buf, slot, which, i=slice(None)):
        rows = buf.shape[3] // 2
        block = buf.at[1, i, :, rows_at(which, rows)]
        return send_to(block, block, kvs.at[slot], kvr.at[slot], section=other)

    def stack(values, n_heads):
        width = values.shape[-1]
        return jnp.concatenate(
            [values * head_mask(width, width // n_heads, h) for h in range(n_heads)], axis=0
        )

    def unstack(values, n_heads):
        rows, width = values.shape[0] // n_heads, values.shape[-1]
        lane = lax.broadcasted_iota(jnp.int32, (1, width), 1)
        out = values[(n_heads - 1) * rows:]
        for h in range(n_heads - 2, -1, -1):
            out = jnp.where(lane < (h + 1) * (width // n_heads), values[h * rows:(h + 1) * rows], out)
        return out

    tile = 32

    def attend(q, k, v, bias, scaling, n_heads, p_ref):
        rows = q.shape[0]
        scores = mm_nt(stack(q, n_heads), k)
        for at in range(0, n_heads * rows, tile):
            low = at % rows
            t = scores[at:at + tile] * (scaling * LOG2E) + bias[low:low + tile]
            e = jnp.exp2(t - jnp.max(t, axis=-1, keepdims=True))
            p = e * reciprocal(jnp.sum(e, axis=-1, keepdims=True))
            p_ref[at:at + tile, :] = p.astype(BF16)
        return unstack(mm(p_ref[...], v), n_heads).astype(BF16)

    def attend_back(q, k, v, o, do, scaling, n_heads, p_ref, ds_ref):
        rows = q.shape[0]
        do_all = stack(do, n_heads)
        o_all = jnp.concatenate([o] * n_heads, axis=0)
        dp = mm_nt(do_all, v)
        for at in range(0, n_heads * rows, tile):
            part = slice(at, at + tile)
            delta = jnp.sum(
                do_all[part].astype(F32) * o_all[part].astype(F32), axis=-1, keepdims=True
            )
            ds_ref[part, :] = (p_ref[part, :].astype(F32) * (dp[part] - delta)).astype(BF16)
        ds = ds_ref[0:n_heads * rows, :]
        dq = unstack(mm(ds, k), n_heads)
        dk = mm_tn(ds, stack(q, n_heads))
        dv = mm_tn(p_ref[...], do_all)
        return dq * scaling, dk * scaling, dv

    def enc_qkv(c, i):
        place, _, keys = spot(c)
        if i == 0:
            ag_wait(h1g, HC, AG_H1, c)
        h1 = h1g[c]
        q_s[i, c] = mm_nt(h1, eqkv[i, 0]).astype(BF16)
        kv_s[keys, i, 0, rows_at(place, n_row), :] = mm_nt(h1, eqkv[i, 1]).astype(BF16)
        kv_s[keys, i, 1, rows_at(place, n_row), :] = mm_nt(h1, eqkv[i, 2]).astype(BF16)

        @pl.when(c == 2)
        def _():
            kv_copy(kv_s, i, s, i).start()

    def members(which):
        return slice(0, 2) if which == 0 else slice(2, 3)

    def half_of(which):
        return (base + s, 0) if which == 0 else (base + 2, s)

    def join(values):
        return values.reshape(values.shape[0] * values.shape[1], values.shape[2])

    def enc_attention(which, i):
        own = members(which)
        mb, place = half_of(which)
        if which == 1:
            kv_copy(kv_s, i, other, i).wait_recv()
        rows = (2 - which) * n_row
        ends = bounds_of(ctx_len, mb)
        qs = segment(lax.broadcasted_iota(jnp.int32, (rows, 1), 0) + place * n_row, ends)
        ks = segment(lax.broadcasted_iota(jnp.int32, (1, n_ctx), 1), ends)
        bias = jnp.where(qs == ks, 0.0, -1e30).astype(F32)
        o = attend(
            join(q_s[i, own]), kv_s[which, i, 0], kv_s[which, i, 1], bias, scale, heads,
            (p_a, p_b)[which].at[i],
        )
        o_s[i, own] = o.reshape(2 - which, n_row, wq)
        if i == 1:
            out = mm(join(o_s[0, own]), eproj[0]) + mm(o, eproj[1])
            part[own] = out.astype(BF16).reshape(2 - which, n_row, W)
            for c in range(own.start, own.stop):
                rs_send(part, rb_o, HC, RS_O, c)

    def enc_second_norm(c):
        rs_copy(part, rb_o, HC, RS_O, c).wait_recv()
        for top in range(0, HC, 16):
            x1 = xin[c, top:top + 16, :].astype(F32) + own_sum(part, rb_o, HC, c, top, 16)
            x1_s[c, top:top + 16, :] = x1
            h2g[c, own_tile(HC, top, 16), :] = norm_forward(x1, en2).astype(BF16)
        ag_send(h2g, HC, AG_H2, c)

    def gelu_tiles(h, weight, a_ref, slope_ref):
        for left in range(0, weight.shape[1], 256):
            right = min(left + 256, weight.shape[1])
            u = mm(h, weight[:, left:right])
            for top in range(0, h.shape[0], 16):
                a, slope = gelu_parts(u[top:top + 16])
                a_ref[top:top + 16, left:right] = a.astype(BF16)
                slope_ref[top:top + 16, left:right] = slope.astype(BF16)

    def slope_tiles(da, weight, slope_ref):
        for left in range(0, weight.shape[0], 256):
            right = min(left + 256, weight.shape[0])
            back = mm_nt(da, weight[left:right, :])
            for top in range(0, da.shape[0], 32):
                at = (slice(top, top + 32), slice(left, right))
                slope_ref[at] = (back[top:top + 32] * slope_ref[at].astype(F32)).astype(BF16)

    def enc_mlp(c, i):
        if i == 0:
            ag_wait(h2g, HC, AG_H2, c)
            rs_copy(part, rb_o, HC, RS_O, c).wait_send()
        gelu_tiles(h2g[c], eup[i], a_s.at[i, c], gp_s.at[i, c])
        total = mm(a_s[i, c], edown[i])
        if i == 1:
            total = total + part[c].astype(F32)
        part[c] = total.astype(BF16)
        if i == 1:
            rs_send(part, rb_a, HC, RS_A, c)

    def p1_copy(c, block):
        at = ph1g.at[c, pl.ds(pl.multiple_of(block * HB, 16), HC)]
        return send_to(at, at, ss.at[AG_P1, c], rs.at[AG_P1, c], mp=x_peer)

    def link_forward(c):
        rs_copy(part, rb_a, HC, RS_A, c).wait_recv()
        for top in range(0, HC, 16):
            out = x1_s[c, top:top + 16, :] + own_sum(part, rb_a, HC, c, top, 16)
            y_s[c, top:top + 16, :] = out.astype(BF16)
        z_s[c] = mm(y_s[c], link[...])
        for top in range(0, HC, 32):
            rows = norm_forward(z_s[c, top:top + 32, :], pn1)
            at = pl.ds(pl.multiple_of(x * HB + top, 16), 32)
            ph1g[c, at, :] = rows.astype(BF16)
        p1_copy(c, x).start()

    def own_first(body, i):
        each(lambda c: body(c, i))

    for n in range(4):
        to_pair(n)
        fetch(n + 4)
    at_hand(0, 1)
    own_first(enc_qkv, 0)
    to_core(0, 1, 2, 3)
    to_pair(4)
    enc_attention(0, 0)
    to_pair(5)
    enc_attention(1, 0)
    each(mask_rows)
    arrived(0, 1, 2)
    own_first(enc_qkv, 1)
    to_core(4)
    to_pair(6)
    arrived(3)
    enc_attention(0, 1)
    to_core(5)
    to_pair(7)
    enc_attention(1, 1)
    fetch(8, 9, 10, 11)

    def second_norm_step(c):
        enc_second_norm(c)

        @pl.when(c == 0)
        def _():
            to_core(6)

        @pl.when(c == 2)
        def _():
            to_core(7)

    each(second_norm_step)
    at_hand(2, 3)
    own_first(enc_mlp, 0)
    arrived(4, 5, 6, 7)
    to_pair(10, 11)
    own_first(enc_mlp, 1)
    to_core(8, 9, 10, 11)
    at_hand(4)
    each(link_forward)

    n_blk = 2 * HB
    n_all = n_mp * HB
    n_tgt = 2 * HT

    def pred_qkv(c):
        place, _, keys = spot(c)
        p1_copy(c, 1 - x).wait_recv()
        h1 = ph1g[c]
        for i in range(2):
            pq_s[i, c] = mm_nt(pt1[c], pqkv[i, 0]).astype(BF16)
            pkv_s[keys, i, 0, rows_at(place, n_blk), :] = mm_nt(h1, pqkv[i, 1]).astype(BF16)
            pkv_s[keys, i, 1, rows_at(place, n_blk), :] = mm_nt(h1, pqkv[i, 2]).astype(BF16)

        @pl.when(c == 2)
        def _():
            kv_copy(pkv_s, 2, s).start()

    def quarters(body):
        def step(i, carry):
            body(i)
            return carry
        lax.fori_loop(0, 2, step, 0)

    def pred_attention(which):
        own = members(which)
        mb, place = half_of(which)
        if which == 1:
            kv_copy(pkv_s, 2, other).wait_recv()
        rows = (2 - which) * n_tgt
        c_ends = bounds_of(ctx_len, mb)
        t_ends = bounds_of(tgt_len, mb)
        qs = segment(lax.broadcasted_iota(jnp.int32, (rows, 1), 0) + place * n_tgt, t_ends)
        row = lax.broadcasted_iota(jnp.int32, (1, n_all), 1)
        block = jnp.zeros((1, n_all), jnp.int32)
        for b in range(1, n_mp):
            block = block + jnp.where(row >= b * HB, 1, 0)
        inner = row - block * HB
        c_seg = segment(block * HC + inner, c_ends)
        t_seg = segment(block * HT + inner - HC, t_ends)
        ks = jnp.where(inner < HC, c_seg, t_seg)
        bias = jnp.where(qs == ks, 0.0, -1e30).astype(F32)
        for i in range(2):
            o = attend(
                join(pq_s[i, own]), pkv_s[which, i, 0], pkv_s[which, i, 1], bias, pscale, pheads,
                (pp_a, pp_b)[which].at[i],
            )
            po_s[i, own] = o.reshape(2 - which, n_tgt, wpq)
        out = mm(join(po_s[0, own]), pproj[0]) + mm(join(po_s[1, own]), pproj[1])
        part_p[own] = out.astype(BF16).reshape(2 - which, n_tgt, PW)
        for c in range(own.start, own.stop):
            ex_copy(part_p, rb_po, RS_PO, c).start()

    def pred_mlp(c):
        ex_wait(part_p, rb_po, RS_PO, c)
        for top in range(0, n_tgt, 32):
            at = slice(top, top + 32)
            x1 = m_s[c, at, :] + ex_sum(part_p, rb_po, c, at)
            px1_s[c, at, :] = x1
            ph2g[c, at, :] = norm_forward(x1, pn2).astype(BF16)
        ag_wait(cotg, HT, AG_COT, c)
        total = jnp.zeros((n_tgt, PW), F32)
        for i in range(2):
            gelu_tiles(ph2g[c], pup[i], pa_s.at[i, c], pdu_s.at[i, c])
            slope_tiles(cotg[c], pdown[i], pdu_s.at[i, c])
            total = total + mm_nt(pdu_s[i, c], pup[i])
        ex_copy(part_p, rb_po, RS_PO, c).wait_send()
        part_p[c] = total.astype(BF16)
        ex_copy(part_p, rb_p2, RS_P2, c).start()

    def dkv_copy(slot, outgoing, incoming):
        return send_to(outgoing, incoming, kvs.at[slot], kvr.at[slot], section=other)

    def pred_second_back(c):
        ex_wait(part_p, rb_p2, RS_P2, c)
        for block in range(2):
            counted = jnp.where(x == block, 1.0, 0.0).astype(F32)
            at = slice(block * HT, (block + 1) * HT)
            dxn, dgain = norm_backward(px1_s[c, at, :], pn2, ex_sum(part_p, rb_p2, c, at))
            dx1 = cotg[c, at, :].astype(F32) + dxn
            pdbg[c, at, :] = dx1.astype(BF16)
            minor_add(3, fold(dgain) * counted)
            minor_add(4, fold(dx1) * counted)

    def pred_attention_back(which):
        own = members(which)
        for c in range(own.start, own.stop):
            pred_second_back(c)

        def one(i):
            do = mm_nt(join(pdbg[own]), pproj[i]).astype(BF16)
            dq, dk, dv = attend_back(
                join(pq_s[i, own]), pkv_s[which, i, 0], pkv_s[which, i, 1], join(po_s[i, own]),
                do, pscale, pheads, (pp_a, pp_b)[which].at[i], pds_s,
            )
            pdq_s[i, own] = dq.astype(BF16).reshape(2 - which, n_tgt, wpq)
            if which == 0:
                pdkv_s[i, own, :, 0:wpq] = dk.astype(BF16).reshape(2, n_blk, wpq)
                pdkv_s[i, own, :, wpq:2 * wpq] = dv.astype(BF16).reshape(2, n_blk, wpq)
            else:
                pdkv_acc[i, 0] = dk
                pdkv_acc[i, 1] = dv

        quarters(one)
        if which == 1:
            pdkv_x[...] = pdkv_acc[:, :, rows_at(other, n_blk), :].astype(BF16)
            dkv_copy(3, pdkv_x, pdkv_r).start()

    def pred_rows_back(c):
        @pl.when(c == 2)
        def _():
            dkv_copy(3, pdkv_x, pdkv_r).wait_recv()
            for i in range(2):
                for which in range(2):
                    total = pdkv_acc[i, which, rows_at(s, n_blk), :] + pdkv_r[i, which].astype(F32)
                    pdkv_s[i, 2, :, which * wpq:(which + 1) * wpq] = total.astype(BF16)

        from_q = jnp.zeros((n_tgt, PW), F32)
        from_kv = jnp.zeros((n_blk, PW), F32)
        for i in range(2):
            from_q = from_q + mm(pdq_s[i, c], pqkv[i, 0])
            from_kv = from_kv + mm(pdkv_s[i, c, :, 0:wpq], pqkv[i, 1])
            from_kv = from_kv + mm(pdkv_s[i, c, :, wpq:2 * wpq], pqkv[i, 2])
        for b in range(2):
            part_p1[c, b * HC:(b + 1) * HC, :] = from_kv[b * HB:b * HB + HC].astype(BF16)
        rs_send(part_p1, rb_p1, HC, RS_P1, c)
        for b in range(2):
            dh1 = from_kv[b * HB + HC:(b + 1) * HB] + from_q[b * HT:(b + 1) * HT]
            dz, dgain = norm_backward(m_s[c, b * HT:(b + 1) * HT, :], pn1, dh1)
            minor_add(2, fold(dgain))
            minor_add(4, fold(dz))

    def pred_first_back(c):
        rs_copy(part_p1, rb_p1, HC, RS_P1, c).wait_recv()
        gain_sum = jnp.zeros((8, PW), F32)
        for top in range(0, HC, 32):
            dh1 = own_sum(part_p1, rb_p1, HC, c, top, 32)
            dz, dgain = norm_backward(z_s[c, top:top + 32, :], pn1, dh1)
            gain_sum = gain_sum + fold(dgain)
            dcg[c, own_tile(HC, top, 32), :] = dz.astype(BF16)
        minor_add(2, gain_sum)
        ag_send(dcg, HC, AG_DY, c)

    at_hand(5, 6, 7, 8)
    arrived(8, 9, 10, 11)
    each(pred_qkv)
    pred_attention(0)
    pred_attention(1)
    each(pred_mlp)
    wgrad(ph2g, pdu_s, 128, (4, 0, 0, PF))
    core_start(4)
    wgrad(cotg, pa_s, 128, (5, 0, 0, PF))
    core_start(5)
    pred_attention_back(1)
    pred_attention_back(0)
    each(pred_rows_back)
    near(4, 5)
    wgrad(pdbg, po_s, 128, (3, 3 * wpq, 0, wpq))
    wgrad(pt1, pdq_s, 128, (3, 0, 0, wpq))
    wgrad(ph1g, pdkv_s, 128, (3, wpq, 0, 2 * wpq))
    core_start(3)
    each(pred_first_back)
    across(4, 5)
    near(3)

    l_right = dcg[:, rows_at(x, HC), :].reshape(nm * HC, PW)

    def link_step(n, carry):
        at = pl.ds(pl.multiple_of(n * 256, 256), 256)
        l_full[at, :] = mm_tn(y_s[:, :, at].reshape(nm * HC, 256), l_right).astype(BF16)
        return carry

    lax.fori_loop(0, W // 256, link_step, 0)
    lh = l_full.shape[0] // 2
    lq = lh // n_mp
    l_core_copy = send_to(
        l_full.at[rows_at(other, lh)], l_core, lcs.at[0], lcr.at[0], section=other
    )
    l_core_copy.start()

    def l_mp_copy(j):
        return send_to(
            l_half.at[rows_at(mp_peer(j), lq)], l_mp.at[j - 1], lms.at[j - 1], lmr.at[j - 1],
            mp=mp_peer(j),
        )

    def l_z_copy(j, slot):
        return send_to(
            l_z.at[slot], l_z.at[slot], lzs.at[j - 1], lzr.at[j - 1], batch=z_peer(j)
        )

    def l_all_copy(j, block):
        at = l_all.at[pl.ds(pl.multiple_of(s * lh + block * lq, lq), lq)]
        return send_to(at, at, las.at[j - 1], lar.at[j - 1], mp=mp_peer(j))

    def l_back_copy(block):
        at = l_all.at[rows_at(block, lh)]
        return send_to(at, at, lcs.at[1], lcr.at[1], section=other)

    def form_dy(c):
        ag_wait(dcg, HC, AG_DY, c)
        dyg[c] = mm_nt(dcg[c], link[...]).astype(BF16)

    def enc_mlp_back(c):
        dy = dyg[c]
        total = jnp.zeros((n_row, W), F32)
        for i in range(2):
            slope_tiles(dy, edown[i], gp_s.at[i, c])
            total = total + mm_nt(gp_s[i, c], eup[i])
        rs_copy(part, rb_a, HC, RS_A, c).wait_send()
        part[c] = total.astype(BF16)
        rs_send(part, rb_2, HC, RS_2, c)

    def enc_second_back(c):
        rs_copy(part, rb_2, HC, RS_2, c).wait_recv()
        gain_sum = jnp.zeros((8, W), F32)
        for top in range(0, HC, 16):
            at = slice(top, top + 16)
            dh2 = own_sum(part, rb_2, HC, c, top, 16)
            dxn, dgain = norm_backward(x1_s[c, at, :], en2, dh2)
            gain_sum = gain_sum + fold(dgain)
            dx1 = dyg[c, own_tile(HC, top, 16), :].astype(F32) + dxn
            dx1_s[c, at, :] = dx1
            dbg[c, own_tile(HC, top, 16), :] = dx1.astype(BF16)
        minor_add(1, gain_sum)
        ag_send(dbg, HC, AG_B, c)

    def enc_attention_back(which):
        own = members(which)
        for c in range(own.start, own.stop):
            ag_wait(dbg, HC, AG_B, c)

        def one(i):
            do = mm_nt(join(dbg[own]), eproj[i]).astype(BF16)
            dq, dk, dv = attend_back(
                join(q_s[i, own]), kv_s[which, i, 0], kv_s[which, i, 1], join(o_s[i, own]), do,
                scale, heads, (p_a, p_b)[which].at[i], ds_s,
            )
            dqkv_s[i, own, :, 0:wq] = dq.astype(BF16).reshape(2 - which, n_row, wq)
            if which == 0:
                dqkv_s[i, own, :, wq:2 * wq] = dk.astype(BF16).reshape(2, n_row, wq)
                dqkv_s[i, own, :, 2 * wq:3 * wq] = dv.astype(BF16).reshape(2, n_row, wq)
            else:
                dkv_acc[i, 0] = dk
                dkv_acc[i, 1] = dv

        quarters(one)
        if which == 1:
            dkv_x[...] = dkv_acc[:, :, rows_at(other, n_row), :].astype(BF16)
            dkv_copy(4, dkv_x, dkv_r).start()

    def enc_shared_keys():
        dkv_copy(4, dkv_x, dkv_r).wait_recv()
        for i in range(2):
            for which in range(2):
                total = dkv_acc[i, which, rows_at(s, n_row), :] + dkv_r[i, which].astype(F32)
                dqkv_s[i, 2, :, (which + 1) * wq:(which + 2) * wq] = total.astype(BF16)

    def enc_rows_back(c):
        total = jnp.zeros((n_row, W), F32)
        for i in range(2):
            for which in range(3):
                total = total + mm(dqkv_s[i, c, :, which * wq:(which + 1) * wq], eqkv[i, which])
        rs_copy(part, rb_2, HC, RS_2, c).wait_send()
        part[c] = total.astype(BF16)
        rs_send(part, rb_1, HC, RS_1, c)

    def dx_same(chunk, slot):
        return send_to(dx_s.at[chunk], dx_r.at[slot], dxs.at[0], dxr.at[slot], section=other)

    def dx_far(chunk, slot, sem):
        return send_to(
            dx_s.at[chunk], dx_r.at[slot], dxs.at[sem], dxr.at[slot], section=y, mp=y_peer
        )

    def enc_first_back(c):
        rs_copy(part, rb_1, HC, RS_1, c).wait_recv()
        gain_sum = jnp.zeros((8, W), F32)
        for top in range(0, HC, 16):
            at = slice(top, top + 16)
            dh1 = own_sum(part, rb_1, HC, c, top, 16)
            dxn, dgain = norm_backward(xin[c, at, :].astype(F32), en1, dh1)
            gain_sum = gain_sum + fold(dgain)
            dx1_s[c, at, :] = dx1_s[c, at, :] + dxn
            dx_s[c, at, :] = dx1_s[c, at, :].astype(BF16)
        minor_add(0, gain_sum)

        @pl.when(jnp.logical_and(s == y, c != 1 - y))
        def _():
            dx_out[0, jnp.where(c == 2, 2, s)] = dx1_s[c]

    def dx_send():
        dx_far(1 - y, s, 1).start()

        @pl.when(s != y)
        def _():
            dx_same(y, s).start()
            dx_far(2, 2, 2).start()

    each(form_dy)
    wgrad(dyg, a_s, 256, (2, 0, 0, FH // 2), (8, 0, FH // 2, FH))
    core_start(2)
    core_start(8)

    def mlp_back_step(c):
        enc_mlp_back(c)

        @pl.when(c == 2)
        def _():
            near(2, 8)
            across(3)

    each(mlp_back_step)
    l_core_copy.wait_recv()

    def l_piece(n, size):
        mine, at = rows_at(4 * s + n, size), rows_at(n, size)
        l_half[at, :] = (l_full[mine, :].astype(F32) + l_core[at, :].astype(F32)).astype(BF16)

    pieces(lh, l_piece)
    for j in range(1, n_mp):
        l_mp_copy(j).start()
    wgrad(h2g, gp_s, 256, (1, 0, 0, FH // 2), (7, 0, FH // 2, FH))
    core_start(1)
    core_start(7)
    each(enc_second_back, 2)
    onward(4, 5)
    total = l_half[rows_at(r, lq), :].astype(F32)
    for j in range(1, n_mp):
        l_mp_copy(j).wait_recv()
        total = total + l_mp[j - 1].astype(F32)
    l_z[z] = total.astype(BF16)
    for j in range(1, nb):
        l_z_copy(j, z).start()
    enc_attention_back(1)
    near(1, 7)
    enc_attention_back(0)
    enc_shared_keys()
    wgrad(dbg, o_s, 256, (6, wq, 0, wq))
    wgrad(h1g, dqkv_s, 256, (6, 0, 2 * wq, 3 * wq))
    core_start(6)
    wgrad(h1g, dqkv_s, 256, (0, 0, 0, 2 * wq))
    core_start(0)
    across(2, 8)
    onward(3)
    for j in range(1, nb):
        l_z_copy(j, z_source(j)).wait_recv()
    total = l_z[0].astype(F32)
    for j in range(1, nb):
        total = total + l_z[j].astype(F32)
    l_all[pl.ds(pl.multiple_of(s * lh + r * lq, lq), lq), :] = total.astype(BF16)
    for j in range(1, n_mp):
        l_all_copy(j, r).start()

    def rows_back_step(c):
        enc_rows_back(c)

        @pl.when(c == 0)
        def _():
            near(6)

        @pl.when(c == 1)
        def _():
            near(0)

    each(rows_back_step)
    each(enc_first_back)

    m_core_copy = send_to(minor, m_core, mcs.at[0], mcr.at[0], section=other)
    m_core_copy.start()

    def m_mp_copy(j, slot):
        return send_to(
            m_mp.at[slot], m_mp.at[slot], mms.at[j - 1], mmr.at[j - 1], mp=mp_peer(j)
        )

    def m_z_copy(j, slot):
        return send_to(
            m_z.at[slot], m_z.at[slot], mzs.at[j - 1], mzr.at[j - 1], batch=z_peer(j)
        )

    across(1, 7)
    onward(2, 8)
    for j in range(1, n_mp):
        l_all_copy(j, mp_source(j)).wait_recv()
    l_back_copy(s).start()
    across(6)
    dx_send()
    onward(1)
    m_core_copy.wait_recv()
    m_mp[r] = minor[...] + m_core[...]
    for j in range(1, n_mp):
        m_mp_copy(j, r).start()
    across(0)
    onward(7)
    for j in range(1, n_mp):
        m_mp_copy(j, mp_source(j)).wait_recv()
    total = m_mp[0]
    for j in range(1, n_mp):
        total = total + m_mp[j]
    m_z[z] = total
    for j in range(1, nb):
        m_z_copy(j, z).start()
    finish(4, 5, 3, 2, 8)
    onward(6)

    def sent(c):
        for buf, rows, ph in (
            (h1g, HC, AG_H1), (h2g, HC, AG_H2), (cotg, HT, AG_COT),
            (dcg, HC, AG_DY), (dbg, HC, AG_B),
        ):
            mine = buf.at[c, rows_at(x, rows)]
            send_to(mine, mine, ss.at[ph, c], rs.at[ph, c], mp=x_peer).wait_send()
        for buf, rb, rows, ph in (
            (part_p1, rb_p1, HC, RS_P1), (part, rb_1, HC, RS_1),
        ):
            rs_copy(buf, rb, rows, ph, c).wait_send()

    each(sent)
    each(lambda c: ex_copy(part_p, rb_p2, RS_P2, c).wait_send())
    each(lambda c: pin_copy(c, x).wait_send())
    each(lambda c: p1_copy(c, x).wait_send())
    for copy in input_copies(0, far + s):
        copy.wait_send()

    @pl.when(s == y)
    def _():
        for copy in input_copies(1, far + 2):
            copy.wait_send()

    dx_far(1 - y, s, 1).wait_send()

    @pl.when(s != y)
    def _():
        dx_same(y, s).wait_send()
        dx_far(2, 2, 2).wait_send()

    for n in range(n_parcel):
        p_far(n).wait_send()
        if n not in DIRECT:
            p_pair(n, pair).wait_send()
        p_swap(n, s).wait_send()
    for i in range(2):
        kv_copy(kv_s, i, s, i).wait_send()
    kv_copy(pkv_s, 2, s).wait_send()
    dkv_copy(3, pdkv_x, pdkv_r).wait_send()
    dkv_copy(4, dkv_x, dkv_r).wait_send()
    l_core_copy.wait_send()
    l_back_copy(s).wait_send()
    m_core_copy.wait_send()
    for j in range(1, n_mp):
        l_mp_copy(j).wait_send()
        l_all_copy(j, r).wait_send()
        m_mp_copy(j, r).wait_send()
    for j in range(1, nb):
        l_z_copy(j, z).wait_send()
        m_z_copy(j, z).wait_send()

    onward(0)
    l_back_copy(other).wait_recv()
    for j in range(1, nb):
        m_z_copy(j, z_source(j)).wait_recv()
    total = m_z[0]
    for j in range(1, nb):
        total = total + m_z[j]
    for i, row in enumerate((0, 1, 4, 2, 3)):
        width = minor_out[i].shape[0]
        minor_out[i][...] = total[row:row + 1, 0:width].reshape(width)

    @pl.when(s == y)
    def _():
        dx_same(y, other).wait_recv()
        dx_out[0, other] = dx_r[other].astype(F32)

    @pl.when(s != y)
    def _():
        for slot in range(3):
            dx_far(1, slot, 1).wait_recv()
            dx_out[0, slot] = dx_r[slot].astype(F32)

    finish(1, 7)

    def grads_sent(*matrices):
        for i in matrices:
            core_copy(i).wait_send()
            for copy in y_copies(i):
                copy.wait_send()
            if z_inside:
                for copy in near_copies(i):
                    copy.wait_send()
                far_copy(i).wait_send()

    grads_sent(1, 2, 3, 4, 5, 7, 8)
    finish(6, 0)
    grads_sent(6, 0)


def hand_over(*refs):
    count = len(refs) // 2
    for src, dst in zip(refs[:count], refs[count:]):
        dst[...] = src[...].astype(dst.dtype)


def body(
    n_mp, nb,
    encoder_in, context_lengths, target_lengths, target_places,
    encoder_norm1, encoder_qkv, encoder_proj, encoder_norm2, encoder_up, encoder_down,
    link_weight, mask_token,
    predictor_norm1, predictor_qkv, predictor_proj, predictor_norm2, predictor_up, predictor_down,
    cotangent,
):
    mb_all, HC, W = encoder_in.shape[1:]
    HT, PW = cotangent.shape[2:]
    HB = HC + HT
    nm = mb_all // 2
    C, T = n_mp * HC, n_mp * HT
    B = n_mp * HB
    wq = encoder_qkv.shape[-1]
    pq = predictor_qkv.shape[-1]
    FH = encoder_up.shape[-1]
    PF = predictor_up.shape[-1]
    heads, pheads = HEADS // n_mp, PHEADS // n_mp
    z_inside = nb == 4 and W // 2 % (16 * nb) == 0 and PW // 2 % (16 * nb) == 0

    g_shapes = [
        (W, 2 * wq), (W, FH // 2), (W, FH // 2), (PW, 4 * pq), (PW, PF), (PW, PF), (W, 2 * wq),
        (W, FH // 2), (W, FH // 2),
    ]
    parts = 2 * nb if z_inside else 2
    a, b = W // parts, PW // parts
    g_outs = [
        (3, a, wq), (wq, a) if z_inside else (a, wq), (a, FH), (a, FH),
        (3, b, pq), (b, pq), (b, PF), (b, PF),
    ]

    def vm(shape, dtype=BF16):
        return pltpu.VMEM(shape, dtype)

    def dma(*shape):
        return pltpu.SemaphoreType.DMA(shape)

    out_shape = (
        [jax.ShapeDtypeStruct((1, nm, HC, W), F32)]
        + [jax.ShapeDtypeStruct(g, F32 if z_inside else BF16) for g in g_outs]
        + [jax.ShapeDtypeStruct((W, PW), BF16)]
        + [jax.ShapeDtypeStruct((width,), F32) for width in (W, W, PW, PW, PW)]
    )
    peers = n_mp - 1
    R, T2, B2 = 2 * HC, 2 * HT, 2 * HB
    acts = [
        vm((nm, HC, W)), vm((nm, HT, PW)), vm((nm, 2, 1, HT), jnp.int32),
        vm((nm, R, W)), vm((2, nm, R, wq)), vm((2, 2, 2, C, wq)), vm((2, nm, R, wq)),
        vm((2, heads * 2 * R, C)), vm((2, heads * R, C)), vm((nm, R, W)), vm((nm, HC, W)), vm((nm, HC, W), F32),
        vm((nm, R, W)), vm((2, nm, R, FH)), vm((2, nm, R, FH)), vm((nm, HC, W)),
        vm((nm, HC, W)), vm((nm, HC, PW), F32), vm((nm, B2, PW)), vm((nm, T2, PW)),
        vm((2, nm, T2, pq)), vm((2, 2, 2, B, pq)), vm((2, nm, T2, pq)),
        vm((2, pheads * 2 * T2, B)), vm((2, pheads * T2, B)), vm((nm, T2, PW)), vm((nm, T2, PW)), vm((nm, T2, PW), F32), vm((nm, T2, PW), F32),
        vm((nm, T2, PW)), vm((2, nm, T2, PF)), vm((nm, T2, PW)), vm((2, nm, T2, PF)),
        vm((nm, T2, PW)), vm((nm, T2, PW)),
        vm((2, nm, T2, pq)), vm((2, nm, B2, 2 * pq)), vm((2, 2, B, pq), F32),
        vm((2, 2, B2, pq)), vm((2, 2, B2, pq)), vm((nm, R, PW)), vm((nm, HC, PW)),
        vm((nm, R, PW)), vm((nm, R, W)), vm((nm, HC, W)),
        vm((nm, HC, W), F32), vm((nm, R, W)), vm((2, nm, R, 3 * wq)), vm((2, 2, C, wq), F32),
        vm((2, 2, R, wq)), vm((2, 2, R, wq)), vm((nm, HC, W)),
        vm((nm, HC, W)), vm((nm, HC, W)), vm((heads * 2 * R, C)), vm((pheads * 2 * T2, B)),
    ]
    assert len(acts) == N_ACT
    weights = [
        jnp.transpose(encoder_qkv, (0, 2, 1)), encoder_proj, encoder_up, encoder_down, link_weight,
        jnp.transpose(predictor_qkv, (0, 2, 1)), predictor_proj, predictor_up, predictor_down,
    ]
    n_weight = len(weights)
    scratch = [vm(w.shape if i == 4 else (2,) + w.shape) for i, w in enumerate(weights)]
    scratch += [dma(n_weight)] + [dma(12)] * 6
    scratch += acts
    scratch += [vm((2, a, b)) for a, b in g_shapes]
    scratch += [vm((2, a // 2, b)) for a, b in g_shapes]
    scratch += [
        vm((2, a // 8, b) if z_inside and i in Z_FIRST else (1, a // 2, b))
        for i, (a, b) in enumerate(g_shapes)
    ]
    scratch += [vm((5, a // 8, b) if z_inside else (1, 16, 128)) for a, b in g_shapes]
    lq = W // 2 // n_mp
    scratch += [
        vm((W, PW)), vm((W // 2, PW)), vm((W // 2, PW)), vm((peers, lq, PW)),
        vm((nb, lq, PW)),
        vm((8, W), F32), vm((8, W), F32), vm((n_mp, 8, W), F32), vm((nb, 8, W), F32),
        dma(N_PHASE, nm), dma(N_PHASE, nm), dma(2, 3), dma(2, 3), dma(2, 3), dma(5), dma(5), dma(3), dma(3),
        dma(9), dma(9), dma(9, 2), dma(9, 2), dma(9, 5), dma(9, 5),
        dma(2), dma(2), dma(peers), dma(peers), dma(nb - 1), dma(nb - 1), dma(peers), dma(peers),
        dma(1), dma(1), dma(peers), dma(peers), dma(nb - 1), dma(nb - 1),
    ]
    in_vmem = pl.BlockSpec(memory_space=pltpu.VMEM)
    anywhere = pl.BlockSpec(memory_space=pl.ANY)
    outs = pl.pallas_call(
        functools.partial(mega, nb, z_inside),
        out_shape=out_shape,
        in_specs=[in_vmem] * 2 + [anywhere] * 3 + [in_vmem] * 5 + [anywhere] * len(weights),
        out_specs=[in_vmem] * len(out_shape),
        scratch_shapes=scratch,
        compiler_params=pltpu.CompilerParams(
            collective_id=0, has_side_effects=True, vmem_limit_bytes=62 * 1024 * 1024
        ),
    )(
        jnp.transpose(context_lengths, (0, 2, 1)),
        jnp.transpose(target_lengths, (0, 2, 1)),
        jnp.transpose(target_places, (1, 0, 2)),
        encoder_in, cotangent,
        encoder_norm1, encoder_norm2, mask_token, predictor_norm1, predictor_norm2,
        *weights,
    )
    if z_inside:
        outs = pl.pallas_call(
            hand_over,
            out_shape=[jax.ShapeDtypeStruct(o.shape, F32) for o in out_shape],
            in_specs=[in_vmem] * len(out_shape),
            out_specs=[in_vmem] * len(out_shape),
        )(*outs)
        grads = outs[1:9]
        eproj = grads[1]
    else:
        outs = [o.astype(F32) for o in outs]
        grads = [
            lax.psum_scatter(g, "batch", scatter_dimension=g.ndim - 2, tiled=True)
            for g in outs[1:9]
        ]
        eproj = grads[1].T
    dx, link_grad = outs[0], outs[9]
    e1, e2, mask_grad, p1, p2 = outs[10:]
    return (
        dx, e1, grads[0], eproj, e2, grads[2], grads[3].T, link_grad, mask_grad,
        p1, grads[4], grads[5].T, p2, grads[6], grads[7].T,
    )


def solution(mesh):
    return jax.shard_map(
        functools.partial(body, mesh.shape["mp"], mesh.shape["batch"]),
        mesh=mesh,
        in_specs=(
            P("batch", None, "mp", None),
            P("batch", None, None),
            P("batch", None, None),
            P("batch", None, "mp"),
            P(),
            P(None, None, "mp"),
            P("mp", None),
            P(),
            P(None, "mp"),
            P("mp", None),
            P(),
            P(),
            P(),
            P(None, None, "mp"),
            P("mp", None),
            P(),
            P(None, "mp"),
            P("mp", None),
            P("batch", None, "mp", None),
        ),
        out_specs=(
            P("batch", "section", "mp", None),
            P(),
            P(None, ("section", "batch"), "mp"),
            P("mp", ("section", "batch")),
            P(),
            P(("section", "batch"), "mp"),
            P("mp", ("section", "batch")),
            P(),
            P(),
            P(),
            P(None, ("section", "batch"), "mp"),
            P("mp", ("section", "batch")),
            P(),
            P(("section", "batch"), "mp"),
            P("mp", ("section", "batch")),
        ),
        check_vma=False,
    )
```

time: 3810 us -> 160 us (0.04)
  waiting for transfers between devices: 1750 us -> 0 us
  blocking collectives: 893 us -> 0 us
  matrix products: 479 us -> 0 us
  local copies, waits for them, and re-layouts: 332 us -> 0 us
  other arithmetic: 257 us -> 0 us
  Pallas kernels: 0 us -> 159 us
    reduce_scatter x76 -> x0, waiting for transfers between devices: 1070 us -> none  [the longest x32 421 us: collect_grads(): lax.psum_scatter(values.astype(jnp.bfloat16), 'mp', scatter_dimension=0,...]
    all_gather x80 -> x0, blocking collectives: 773 us -> none  [the longest x48 466 us: spread_rows(): return lax.all_gather(values, 'mp', axis=0, tiled=True)]
    dot_general x312 -> x0, matrix products: 459 us -> none  [the longest x16 66.3 us: block_backward(): jnp.dot(hidden.T, grad_branch, preferred_element_type=jnp.float32)]
    while x103 -> x0, waiting for transfers between devices: 362 us -> none
    psum x3 -> x0, waiting for transfers between devices: 315 us -> none  [reduce_step(): minor_part = lax.psum(minor_item, ('section', 'batch', 'mp'))]
    reduce_sum x204 -> x0, other arithmetic: 166 us -> none  [the longest x14 45.2 us: pair_up(): jnp.sum(part_arr.reshape((half_count, 2) + part_arr.shape[1:]), axis=1)]
    pallas_call x0 -> x2, Pallas kernels: none -> 159 us  [the longest x1 155 us: body(): pl.pallas_call(functools.partial(mega, nb, z_inside), out_shape=out_shape...]
    psum x3 -> x0, blocking collectives: 120 us -> none  [reduce_step(): minor_part = lax.psum(minor_item, ('section', 'batch', 'mp'))]
  transfers between devices with their start and end apart: 108 -> 0, of which waited for: 56 -> 0; matrix products, arithmetic and copies ran while one was open for 23% -> 0% of each run, Pallas kernels for 0% -> 0%
where the time goes in v1:
time: 160 us
  Pallas kernels  159 us (99%)
    pallas_call x1, Pallas kernels, body(): pl.pallas_call(functools.partial(mega, nb, z_inside), out_shape=out_shape...  155 us
    pallas_call x1, Pallas kernels, body(): pl.pallas_call(hand_over, out_shape=[jax.ShapeDtypeStruct(o.shape, F32) f...  3.28 us

profile of v1, /device:TPU:0, one launch (start us, length us, event | category | flops | bytes accessed | tf_op | source)
XLA Modules:
  0.0 159.6 jit_solution(15528461224129835347)
XLA Ops:
  0.7 155.5 %shard_map.298 = (f32[1,3,64,768]{3,2,1,0:T(8,128)}, f32[3,96,192]{2,1,0:T(8,128)}, f32[192,96]{1,0:T(8,128)}, f32[96,768]{1,0:T(8,128)}, f32[96,768]{1,0:T(8,12...) custom-call(s32[1,4,6]{2,1,0:T(4,128)} %bitcast.11, ...), custom_call_target="tpu_custom_call" | custom-call | tf_op jit(solution)/shard_map/pallas_call | solution.py:1403
  156.2 3.3 %shard_map.299 = (f32[1,3,64,768]{3,2,1,0:T(8,128)}, f32[3,96,192]{2,1,0:T(8,128)}, f32[192,96]{1,0:T(8,128)}, f32[96,768]{1,0:T(8,128)}, f32[96,768]{1,0:T(8,12...) custom-call(f32[1,3,64,768]{3,2,1,0:T(8,128)} %get-tuple-element.45., ...), custom_call_target="tpu_custom_call" | custom-call | tf_op jit(solution)/shard_map/pallas_call | solution.py:1421
